TPU v7x, 32 devices: a whole 2x2x4 slice. The times are simulated.
32 devices in a mesh: section: 2 (over x), expert: 4 (over z), dp: 4 (over y, core).
Axes of the slice: x: 2, y: 2, z: 4, core: 2. Of those that a mesh axis runs over, the one named last changes fastest.
Arguments:
- frames: bfloat16 [4, 32, 48, 1280], P(None, ('expert', 'dp')), may hold values from -6 to 6
- norm_gain: float32 [2, 1280], P('section'), may hold values from 0.1 to 1.9
- router: bfloat16 [2, 1280, 4], P('section'), may hold values from -0.15625 to 0.15625
- w_in: bfloat16 [2, 4, 1280, 256], P('section', 'expert'), may hold values from -0.15625 to 0.15625
- w_out: bfloat16 [2, 4, 256, 1280], P('section', 'expert'), may hold values from -0.375 to 0.375
- routing: int32 [2, 4, 32, 48, 1], P('section', None, ('expert', 'dp')), may hold values from 0 to 3; in each aligned block of 96 rows (0 to 95, 96 to 191, ..., all dimensions but the last counted through in order) at most 27 rows name the same one
- head_gain: float32 [1280], replicated, may hold values from 0.1 to 1.9
- head_weight: bfloat16 [1280, 8000], P(None, 'expert'), may hold values from -6 to 6
- frame_lengths: int32 [4, 32], P(None, ('expert', 'dp')), may hold values from 24 to 48
- labels: int32 [4, 32, 12], P(None, ('expert', 'dp')), may hold values from 1 to 7999
- label_lengths: int32 [4, 32], P(None, ('expert', 'dp')), may hold values from 1 to 12
Outputs:
- losses: float32 [8, 16], P('section', ('expert', 'dp'))
- head_grad: bfloat16 [1280, 8000], P(None, 'expert')
Inputs may be any that keep to these rules, and one draw needn't show every extreme that they name: `routing`: in each layer and micro-batch, within the frames of one device (aligned blocks of 96 frames), no expert is named by more than 27 frames.
All inputs are finite; a program needn't handle non-finite values.
Results may differ from a plain program's by a relative error of at most 0.015.
Values may be sent and summed in bfloat16 or wider, within the bound.
No kernel may reach another device: no remote copies, remote signals or barrier semaphores. Data moves between devices by JAX's collectives and lax.ppermute only.
A program may use at most 64 MiB of HBM per device.

v0:
```python
import jax
import jax.numpy as jnp
import numpy as np
from jax import lax
from jax.experimental import pallas as pl
from jax.experimental.pallas import tpu as pltpu
from jax.sharding import Mesh, PartitionSpec as P

EPSILON = 1e-06
LOG_ZERO = -1e30
VMEM_LIMIT = 24 * 1024 * 1024
LANES = 128
COLS = 16
PEAK, TOTAL, WHOLE = COLS - 3, COLS - 2, COLS - 3
BLOCK_ROWS = 256
NT = (((1,), (1,)), ((), ()))
NN = (((1,), (0,)), ((), ()))


def round_up(value, unit):
    return -(-value // unit) * unit


def vmem_spec():
    return pl.BlockSpec(memory_space=pltpu.VMEM)


def smem_spec():
    return pl.BlockSpec(memory_space=pltpu.SMEM)


def call(kernel, out_shape, flops=0, moved=0, **options):
    return pl.pallas_call(
        kernel,
        out_shape=out_shape,
        compiler_params=pltpu.CompilerParams(vmem_limit_bytes=VMEM_LIMIT),
        cost_estimate=pl.CostEstimate(flops=flops, bytes_accessed=moved, transcendentals=0),
        **options,
    )


def bf16_rows(count, width):
    return jax.ShapeDtypeStruct((count, width), jnp.bfloat16)


def as_mask(values):
    return values.astype(jnp.float32).astype(jnp.bfloat16)


def rms_scale(values, gain):
    values = values.astype(jnp.float32)
    scale = lax.rsqrt(jnp.mean(values * values, axis=-1, keepdims=True) + EPSILON)
    return (values * scale * gain).astype(jnp.bfloat16)


def expert_column(ids, frame_count):
    pairs = ids.shape[0]
    square = jnp.concatenate(
        [ids.astype(jnp.float32), jnp.full((LANES - pairs, LANES), -1.0, jnp.float32)], axis=0
    )
    turned = jnp.transpose(square, (1, 0)).astype(jnp.int32)
    return jnp.concatenate([turned[:frame_count, p : p + 1] for p in range(pairs)], axis=0)


def placement(column, member, experts, capacity):
    count = column.shape[0]
    shifted = column - member
    relative = jnp.where(shifted < 0, shifted + experts, shifted)
    lane = lax.broadcasted_iota(jnp.int32, (count, LANES), 1)
    one_hot = (lane == relative).astype(jnp.float32)
    before = lax.broadcasted_iota(jnp.int32, (count, count), 1) <= lax.broadcasted_iota(
        jnp.int32, (count, count), 0
    )
    rank = lax.dot_general(
        as_mask(before), one_hot.astype(jnp.bfloat16), NN, preferred_element_type=jnp.float32
    )
    start = (lane * capacity - 1).astype(jnp.float32)
    slots = jnp.sum(one_hot * (rank + start), axis=1, keepdims=True).astype(jnp.int32)
    places = lax.broadcasted_iota(jnp.int32, (count, experts * capacity), 1)
    return (places == slots).astype(jnp.float32)


def scatter_rows(rows, ids, member, experts, capacity, frame_count, out_refs):
    count = rows.shape[0]
    chosen = placement(expert_column(ids, frame_count), member, experts, capacity)
    tall = round_up(count, LANES)
    if tall > count:
        chosen = jnp.concatenate(
            [chosen, jnp.zeros((tall - count, chosen.shape[1]), jnp.float32)], axis=0
        )
    pick = jnp.transpose(chosen, (1, 0))[:, :count].astype(jnp.bfloat16)
    placed = lax.dot_general(pick, rows, NN, preferred_element_type=jnp.float32).astype(
        jnp.bfloat16
    )
    for turn, out_ref in enumerate(out_refs):
        out_ref[...] = placed[turn * capacity : (turn + 1) * capacity]


def combine_rows(rows, returned, ids, table, member, experts, capacity, frame_count):
    column = expert_column(ids, frame_count)
    pick = placement(column, member, experts, capacity).astype(jnp.bfloat16)
    normed = rms_scale(rows, table[:1])
    router = jnp.concatenate(
        [table[8:], jnp.zeros((LANES + 8 - table.shape[0], rows.shape[1]), jnp.float32)], axis=0
    ).astype(jnp.bfloat16)
    logits = lax.dot_general(normed, router, NT, preferred_element_type=jnp.float32)
    lane = lax.broadcasted_iota(jnp.int32, logits.shape, 1)
    gate = jax.nn.sigmoid(jnp.sum(jnp.where(lane == column, logits, 0.0), axis=1, keepdims=True))
    stacked = jnp.concatenate(returned, axis=0)
    mixed = lax.dot_general(pick, stacked, NN, preferred_element_type=jnp.float32)
    return (rows.astype(jnp.float32) + gate * mixed).astype(jnp.bfloat16)


def dispatch(rows, ids, member, experts, capacity, frame_count):
    width = rows.shape[1]

    def kernel(member_ref, rows_ref, ids_ref, *out_refs):
        scatter_rows(
            rows_ref[...], ids_ref[...], member_ref[0], experts, capacity, frame_count, out_refs
        )

    return call(
        kernel,
        tuple(bf16_rows(capacity, width) for _ in range(experts)),
        1 << 27,
        1 << 20,
        in_specs=[smem_spec()] + [vmem_spec()] * 2,
        out_specs=tuple(vmem_spec() for _ in range(experts)),
    )(member, rows, ids)


def run_expert(received, table, own, other, pick_own):
    count = len(received)
    capacity, width = received[0].shape
    others = len(other)

    def kernel(pick_ref, table_ref, in_ref, out_weight_ref, *refs):
        other_refs, received_refs, out_refs = (
            refs[: 2 * others],
            refs[2 * others : 2 * others + count],
            refs[2 * others + count :],
        )

        def work(pieces):
            stacked = jnp.concatenate([ref[...] for ref in received_refs], axis=0)
            normed = rms_scale(stacked, table_ref[:1])
            total = None
            for weight_in, weight_out in pieces:
                hidden = lax.dot_general(
                    normed, weight_in[...], NN, preferred_element_type=jnp.float32
                )
                active = (hidden / (1.0 + jnp.exp(-hidden))).astype(jnp.bfloat16)
                part = lax.dot_general(
                    active, weight_out[...], NN, preferred_element_type=jnp.float32
                )
                total = part if total is None else total + part
            total = total.astype(jnp.bfloat16)
            for turn, out_ref in enumerate(out_refs):
                out_ref[...] = total[turn * capacity : (turn + 1) * capacity]

        if others == 0:
            work([(in_ref, out_weight_ref)])
            return

        @pl.when(pick_ref[0] == 1)
        def _():
            work([(in_ref, out_weight_ref)])

        @pl.when(pick_ref[0] != 1)
        def _():
            work([(other_refs[2 * i], other_refs[2 * i + 1]) for i in range(others)])

    flat = [weight for pair in other for weight in pair]
    return call(
        kernel,
        tuple(bf16_rows(capacity, width) for _ in range(count)),
        4 * count * capacity * width * own[0].shape[1],
        4 << 20,
        in_specs=[smem_spec()] + [vmem_spec()] * (3 + 2 * others + count),
        out_specs=tuple(vmem_spec() for _ in range(count)),
    )(pick_own, table, *own, *flat, *received)


def combine_and_dispatch(
    rows, returned, ids, table, next_ids, member, experts, capacity, frame_count
):
    width = rows.shape[1]

    def kernel(member_ref, rows_ref, ids_ref, table_ref, next_ref, *refs):
        returned_refs, x_ref, out_refs = refs[:experts], refs[experts], refs[experts + 1 :]
        mixed = combine_rows(
            rows_ref[...],
            [ref[...] for ref in returned_refs],
            ids_ref[...],
            table_ref[...],
            member_ref[0],
            experts,
            capacity,
            frame_count,
        )
        x_ref[...] = mixed
        scatter_rows(
            mixed, next_ref[...], member_ref[0], experts, capacity, frame_count, out_refs
        )

    shapes = (bf16_rows(*rows.shape),) + tuple(
        bf16_rows(capacity, width) for _ in range(experts)
    )
    result = call(
        kernel,
        shapes,
        1 << 28,
        2 << 20,
        in_specs=[smem_spec()] + [vmem_spec()] * (4 + experts),
        out_specs=tuple(vmem_spec() for _ in shapes),
    )(member, rows, ids, table, next_ids, *returned)
    return result[0], result[1:]


def combine_and_norm(
    rows, returned, ids, table, head_gain, member, experts, capacity, frame_count
):
    def kernel(member_ref, rows_ref, ids_ref, table_ref, head_ref, *refs):
        final = combine_rows(
            rows_ref[...],
            [ref[...] for ref in refs[:experts]],
            ids_ref[...],
            table_ref[...],
            member_ref[0],
            experts,
            capacity,
            frame_count,
        )
        refs[experts][...] = rms_scale(final, head_ref[...])

    return call(
        kernel,
        bf16_rows(*rows.shape),
        1 << 28,
        2 << 20,
        in_specs=[smem_spec()] + [vmem_spec()] * (4 + experts),
        out_specs=vmem_spec(),
    )(member, rows, ids, table, head_gain, *returned)


def label_rows(weight, places):
    shard, width = weight.shape
    entries = places.shape[0]
    blocks = -(-shard // BLOCK_ROWS)

    def kernel(places_ref, weight_ref, out_ref, total_ref):
        step = pl.program_id(0)
        inside = (
            step * BLOCK_ROWS + lax.broadcasted_iota(jnp.int32, (BLOCK_ROWS, 1), 0) < shard
        )
        entry = step * BLOCK_ROWS + lax.broadcasted_iota(jnp.int32, (entries, BLOCK_ROWS), 1)
        values = jnp.where(inside, weight_ref[...].astype(jnp.float32), 0.0).astype(jnp.bfloat16)
        part = lax.dot_general(
            as_mask(entry == places_ref[...]), values, NN, preferred_element_type=jnp.float32
        )

        @pl.when(step == 0)
        def _():
            total_ref[...] = part

        @pl.when(step > 0)
        def _():
            total_ref[...] += part

        @pl.when(step == blocks - 1)
        def _():
            out_ref[...] = total_ref[...].astype(jnp.bfloat16)

    return call(
        kernel,
        bf16_rows(entries, width),
        2 * blocks * BLOCK_ROWS * entries * width,
        6 << 20,
        grid=(blocks,),
        in_specs=[
            pl.BlockSpec((entries, 1), lambda i: (0, 0)),
            pl.BlockSpec((BLOCK_ROWS, width), lambda i: (i, 0)),
        ],
        out_specs=pl.BlockSpec((entries, width), lambda i: (0, 0)),
        scratch_shapes=[pltpu.VMEM((entries, width), jnp.float32)],
    )(places, weight)


def head_logits(pieces, weight, label_weight, frame_count):
    count = len(pieces)
    span, width = pieces[0].shape
    row_count = count * span
    shard = weight.shape[0]
    blocks = -(-shard // BLOCK_ROWS)
    used = shard - (blocks - 1) * BLOCK_ROWS
    entries = label_weight.shape[0]

    def kernel(weight_ref, label_ref, *refs):
        piece_refs = refs[:count]
        logits_ref, rows_ref, stats_ref, peak_ref, total_ref = refs[count:]
        step = pl.program_id(0)

        @pl.when(step == 0)
        def _():
            for slot in range(count):
                rows_ref[slot * span : (slot + 1) * span] = piece_refs[slot][...]
            peak_ref[...] = jnp.full(peak_ref.shape, LOG_ZERO, jnp.float32)
            total_ref[...] = jnp.zeros(total_ref.shape, jnp.float32)

        logits_ref[...] = lax.dot_general(
            weight_ref[...], rows_ref[...], NT, preferred_element_type=jnp.float32
        )
        if used < BLOCK_ROWS:

            @pl.when(step == blocks - 1)
            def _():
                logits_ref[used:] = jnp.full((BLOCK_ROWS - used, row_count), LOG_ZERO, jnp.float32)

        logits = logits_ref[...]
        before = peak_ref[...]
        peak = jnp.maximum(before, jnp.max(logits, axis=0, keepdims=True))
        total_ref[...] = total_ref[...] * jnp.exp(before - peak) + jnp.sum(
            jnp.exp(logits - peak), axis=0, keepdims=True
        )
        peak_ref[...] = peak

        @pl.when(step == blocks - 1)
        def _():
            crossed = lax.dot_general(
                label_ref[...], rows_ref[...], NT, preferred_element_type=jnp.float32
            )
            owner = lax.broadcasted_iota(jnp.int32, (COLS, row_count), 1) // frame_count
            picked = jnp.zeros((COLS, row_count), jnp.float32)
            for utterance in range(entries // COLS):
                part = crossed[utterance * COLS : (utterance + 1) * COLS]
                picked = picked + jnp.where(owner == utterance, part, 0.0)
            place = lax.broadcasted_iota(jnp.int32, (COLS, row_count), 0)
            stats = jnp.where(place == PEAK, peak_ref[...], picked)
            stats = jnp.where(place == TOTAL, total_ref[...], stats)
            for slot in range(count):
                stats_ref[slot] = stats[:, slot * span : (slot + 1) * span]

    return call(
        kernel,
        (
            jax.ShapeDtypeStruct((blocks * BLOCK_ROWS, row_count), jnp.float32),
            bf16_rows(row_count, width),
            jax.ShapeDtypeStruct((count, COLS, span), jnp.float32),
        ),
        2 * blocks * BLOCK_ROWS * row_count * width,
        9 << 20,
        grid=(blocks,),
        in_specs=[
            pl.BlockSpec((BLOCK_ROWS, width), lambda i: (i, 0)),
            pl.BlockSpec((entries, width), lambda i: (0, 0)),
        ]
        + [pl.BlockSpec((span, width), lambda i: (0, 0))] * count,
        out_specs=(
            pl.BlockSpec((BLOCK_ROWS, row_count), lambda i: (i, 0)),
            pl.BlockSpec((row_count, width), lambda i: (0, 0)),
            pl.BlockSpec((count, COLS, span), lambda i: (0, 0, 0)),
        ),
        scratch_shapes=[
            pltpu.VMEM((1, row_count), jnp.float32),
            pltpu.VMEM((1, row_count), jnp.float32),
        ],
    )(weight, label_weight, *pieces)


def log_add(first, second):
    peak = jnp.maximum(first, second)
    return peak + jnp.log(jnp.exp(first - peak) + jnp.exp(second - peak))


def log_add3(first, second, third):
    peak = jnp.maximum(jnp.maximum(first, second), third)
    return peak + jnp.log(
        jnp.exp(first - peak) + jnp.exp(second - peak) + jnp.exp(third - peak)
    )


def ctc_pass(stats, slots, labels, frame_counts, label_counts, frame_count, label_max):
    sources = len(stats)
    count, _, span = stats[0].shape
    row_count = count * span
    utterances = labels.shape[0]
    entries = utterances * COLS

    def kernel(slots_ref, labels_ref, frames_ref, counts_ref, *refs):
        stats_refs = refs[:sources]
        (
            out_ref,
            high_ref,
            low_ref,
            loss_ref,
            turn_ref,
            emission_ref,
            blank_fwd,
            label_fwd,
            blank_bwd,
            label_bwd,
            occupancy_ref,
        ) = refs[sources:]
        place = lax.broadcasted_iota(jnp.int32, (COLS, span), 0)
        turn_ref[...] = jnp.zeros(turn_ref.shape, jnp.float32)
        for slot in range(count):
            found = [stats_refs[k][slots_ref[k * count + slot]] for k in range(sources)]
            joined = found[0]
            peak = found[0][PEAK : PEAK + 1]
            for part in found[1:]:
                joined = joined + part
                peak = jnp.maximum(peak, part[PEAK : PEAK + 1])
            total = jnp.zeros((1, span), jnp.float32)
            for part in found:
                total = total + part[TOTAL : TOTAL + 1] * jnp.exp(part[PEAK : PEAK + 1] - peak)
            log_total = peak + jnp.log(total)
            turn_ref[:COLS, :span] = jnp.where(place == TOTAL, log_total, joined - log_total)
            emission_ref[slot * span : (slot + 1) * span] = jnp.transpose(turn_ref[...], (1, 0))[
                :span
            ]

        lane = lax.broadcasted_iota(jnp.int32, (utterances, 128), 1)
        is_label = lane < label_max
        is_blank = lane <= label_max
        names = labels_ref[...]
        earlier = pltpu.roll(names, 1, 1)
        skip = is_label & (lane >= 1) & (names != 0) & (names != earlier)
        later = pltpu.roll(names, 127, 1)
        skip_next = (lane < label_max - 1) & (later != 0) & (later != names)
        frames = frames_ref[...]
        counts = counts_ref[...]
        lowest = jnp.full((utterances, 128), LOG_ZERO, jnp.float32)
        ends_blank = jnp.where(lane == counts, 0.0, LOG_ZERO)
        ends_label = jnp.where(lane == counts - 1, 0.0, LOG_ZERO)

        def emitted(step):
            row = emission_ref[pl.ds(step, utterances, stride=frame_count), :]
            blank = jnp.sum(jnp.where(lane == label_max, row, 0.0), axis=1, keepdims=True)
            return (
                jnp.where(is_blank, blank, LOG_ZERO),
                jnp.where(is_label, row, LOG_ZERO),
            )

        def advance(step, carry):
            fwd_blank, fwd_label, bwd_blank, bwd_label = carry
            emit_blank, emit_label = emitted(step)
            moved = jnp.where(lane == 0, LOG_ZERO, pltpu.roll(fwd_label, 1, 1))
            new_blank = log_add(fwd_blank, moved) + emit_blank
            new_label = (
                log_add3(fwd_label, fwd_blank, jnp.where(skip, moved, LOG_ZERO)) + emit_label
            )
            start_blank = jnp.where(lane == 0, emit_blank, LOG_ZERO)
            start_label = jnp.where(lane == 0, emit_label, LOG_ZERO)
            first = step == 0
            new_blank = jnp.where(first, start_blank, new_blank)
            new_label = jnp.where(first, start_label, new_label)
            alive = step < frames
            fwd_blank = jnp.where(alive, jnp.where(is_blank, new_blank, LOG_ZERO), fwd_blank)
            fwd_label = jnp.where(alive, jnp.where(is_label, new_label, LOG_ZERO), fwd_label)
            blank_fwd[step] = fwd_blank
            label_fwd[step] = fwd_label

            back = frame_count - 1 - step
            emit_blank, emit_label = emitted(jnp.minimum(back + 1, frame_count - 1))
            out_blank = bwd_blank + emit_blank
            out_label = bwd_label + emit_label
            next_blank = pltpu.roll(out_blank, 127, 1)
            next_label = jnp.where(skip_next, pltpu.roll(out_label, 127, 1), LOG_ZERO)
            new_blank = log_add(out_blank, out_label)
            new_label = log_add3(out_label, next_blank, next_label)
            last = back == frames - 1
            inside = back < frames - 1
            bwd_blank = jnp.where(last, ends_blank, jnp.where(inside, new_blank, LOG_ZERO))
            bwd_label = jnp.where(last, ends_label, jnp.where(inside, new_label, LOG_ZERO))
            bwd_blank = jnp.where(is_blank, bwd_blank, LOG_ZERO)
            bwd_label = jnp.where(is_label, bwd_label, LOG_ZERO)
            blank_bwd[back] = bwd_blank
            label_bwd[back] = bwd_label
            return (fwd_blank, fwd_label, bwd_blank, bwd_label)

        fwd_blank, fwd_label, _, _ = lax.fori_loop(
            0, frame_count, advance, (lowest, lowest, lowest, lowest)
        )
        end_state = jnp.sum(jnp.where(lane == counts, fwd_blank, 0.0), axis=1, keepdims=True)
        near_state = jnp.sum(jnp.where(lane == counts - 1, fwd_label, 0.0), axis=1, keepdims=True)
        log_like = log_add(end_state, near_state)
        loss_ref[...] = jnp.broadcast_to(-log_like, (utterances, 128))

        def occupy(step, carry):
            alive = step < frames
            blank = jnp.exp(blank_fwd[step] + blank_bwd[step] - log_like)
            label = jnp.exp(label_fwd[step] + label_bwd[step] - log_like)
            blank = jnp.sum(jnp.where(is_blank, blank, 0.0), axis=1, keepdims=True)
            label = jnp.where(is_label, label, 0.0)
            whole = blank + jnp.sum(label, axis=1, keepdims=True)
            filled = jnp.where(lane == label_max, blank, label)
            filled = jnp.where(lane == WHOLE, whole, filled)
            filled = jnp.where(alive, -filled, 0.0)
            row = emission_ref[pl.ds(step, utterances, stride=frame_count), :]
            occupancy_ref[pl.ds(step, utterances, stride=frame_count), :] = jnp.where(
                lane == TOTAL, row, filled
            )
            return carry

        lax.fori_loop(0, frame_count, occupy, 0, unroll=8)
        turned = jnp.transpose(occupancy_ref[...], (1, 0))[:COLS]
        out_ref[...] = turned
        row_place = lax.broadcasted_iota(jnp.int32, (COLS, row_count), 0)
        owner = lax.broadcasted_iota(jnp.int32, (COLS, row_count), 1) // frame_count
        source = jnp.where(row_place < WHOLE, turned, 0.0)
        for utterance in range(utterances):
            part = jnp.where(owner == utterance, source, 0.0)
            high = part.astype(jnp.bfloat16)
            high_ref[utterance * COLS : (utterance + 1) * COLS] = high
            low_ref[utterance * COLS : (utterance + 1) * COLS] = (
                part - high.astype(jnp.float32)
            ).astype(jnp.bfloat16)

    held = pltpu.VMEM((frame_count, utterances, 128), jnp.float32)
    return call(
        kernel,
        (
            jax.ShapeDtypeStruct((COLS, row_count), jnp.float32),
            bf16_rows(entries, row_count),
            bf16_rows(entries, row_count),
            jax.ShapeDtypeStruct((utterances, 128), jnp.float32),
        ),
        1 << 26,
        1 << 20,
        in_specs=[smem_spec()] + [vmem_spec()] * (3 + sources),
        out_specs=tuple(vmem_spec() for _ in range(4)),
        scratch_shapes=[
            pltpu.VMEM((128, 128), jnp.float32),
            pltpu.VMEM((row_count, 128), jnp.float32),
            held,
            held,
            held,
            held,
            pltpu.VMEM((row_count, 128), jnp.float32),
        ],
    )(slots, labels, frame_counts, label_counts, *stats)


def head_gradient(groups, order, blocks):
    count = len(groups)
    row_count, width = groups[0]["rows"].shape
    entries = groups[0]["places"].shape[1]
    names = ("logits", "rows", "out", "high", "low", "places")

    def kernel(order_ref, *refs):
        out_ref, rows_ref = refs[count * len(names) :]
        sets = [
            dict(zip(names, refs[g * len(names) : (g + 1) * len(names)])) for g in range(count)
        ]
        step = pl.program_id(0)

        @pl.when(step == 0)
        def _():
            for g, held in enumerate(sets):
                rows_ref[g * row_count : (g + 1) * row_count] = held["rows"][...]

        entry = order_ref[step] * BLOCK_ROWS + lax.broadcasted_iota(
            jnp.int32, (BLOCK_ROWS, entries), 0
        )
        grads = []
        for held in sets:
            select = as_mask(entry == held["places"][...])
            scattered = lax.dot_general(
                select, held["high"][...], NN, preferred_element_type=jnp.float32
            ) + lax.dot_general(select, held["low"][...], NN, preferred_element_type=jnp.float32)
            whole = held["out"][WHOLE : WHOLE + 1]
            log_total = held["out"][TOTAL : TOTAL + 1]
            grad = scattered - jnp.exp(held["logits"][...] - log_total) * whole
            grads.append(grad.astype(jnp.bfloat16))
        out_ref[...] = lax.dot_general(
            jnp.concatenate(grads, axis=1),
            rows_ref[...],
            NN,
            preferred_element_type=jnp.float32,
        ).astype(jnp.bfloat16)

    specs = [
        pl.BlockSpec((BLOCK_ROWS, row_count), lambda i, order: (order[i], 0)),
        pl.BlockSpec((row_count, width), lambda i, order: (0, 0)),
        pl.BlockSpec((COLS, row_count), lambda i, order: (0, 0)),
        pl.BlockSpec((entries, row_count), lambda i, order: (0, 0)),
        pl.BlockSpec((entries, row_count), lambda i, order: (0, 0)),
        pl.BlockSpec((1, entries), lambda i, order: (0, 0)),
    ]
    return call(
        kernel,
        bf16_rows(blocks * BLOCK_ROWS, width),
        2 * blocks * BLOCK_ROWS * row_count * count * (width + 2 * entries),
        10 << 20,
        grid_spec=pltpu.PrefetchScalarGridSpec(
            num_scalar_prefetch=1,
            grid=(blocks,),
            in_specs=specs * count,
            out_specs=pl.BlockSpec((BLOCK_ROWS, width), lambda i, order: (i, 0)),
            scratch_shapes=[pltpu.VMEM((count * row_count, width), jnp.bfloat16)],
        ),
    )(order, *[group[name] for group in groups for name in names])


def assemble(pieces, offsets, height):
    count = len(pieces)
    part, width = pieces[0].shape
    short = height % part

    def kernel(offsets_ref, *refs):
        out_ref, sems = refs[count], refs[count + 1]

        def each(act):
            for index in range(count):
                offset = pl.multiple_of(offsets_ref[index], part)

                @pl.when(offset + part <= height)
                def _():
                    act(
                        pltpu.make_async_copy(
                            refs[index], out_ref.at[pl.ds(offset, part)], sems.at[index]
                        )
                    )

                if short:

                    @pl.when(offset + part > height)
                    def _():
                        act(
                            pltpu.make_async_copy(
                                refs[index].at[pl.ds(0, short)],
                                out_ref.at[pl.ds(height - short, short)],
                                sems.at[index],
                            )
                        )

        each(lambda copy: copy.start())
        each(lambda copy: copy.wait())

    return call(
        kernel,
        bf16_rows(height, width),
        0,
        2 * height * width * 2,
        in_specs=[smem_spec()] + [pl.BlockSpec(memory_space=pl.ANY)] * count,
        out_specs=pl.BlockSpec(memory_space=pl.ANY),
        scratch_shapes=[pltpu.SemaphoreType.DMA((count,))],
    )(offsets, *pieces)


def swap(value, axis):
    return lax.ppermute(value, axis, [(0, 1), (1, 0)])


def rotate(value, axis, by):
    count = lax.axis_size(axis)
    return lax.ppermute(value, axis, [(i, (i + by) % count) for i in range(count)])


def spread_rows(value, member):
    left = lax.ppermute(value, "expert", [(1, 0), (2, 1), (3, 2)])
    right = lax.ppermute(value, "expert", [(0, 1), (1, 2), (2, 3)])
    left_far = lax.ppermute(left, "expert", [(1, 0), (2, 1)])
    right_far = lax.ppermute(right, "expert", [(1, 2), (2, 3)])
    low = member < 2
    near = jnp.where(low, left, right)
    far = jnp.where(low, left_far, right_far)
    end = lax.ppermute(far, "expert", [(1, 0), (2, 3)])
    passed = jnp.where(low, right, left)
    last = jnp.where((member == 0) | (member == 3), end, passed)
    return [value, near, far, last]


LINE_ORDER = np.array([[0, 1, 2, 3], [1, 2, 3, 0], [2, 1, 0, 3], [3, 2, 1, 0]])


def slot_orders(count):
    return LINE_ORDER if count == 4 else np.tile(np.arange(count), (count, 1))


def slot_tables(count):
    orders = slot_orders(count)
    tables = np.zeros((count, count, count), np.int32)
    for member in range(count):
        for k in range(count):
            source = (member + k) % count
            for slot in range(count):
                tables[member, k, slot] = list(orders[source]).index(orders[member][slot])
    return tables.reshape(count, count * count)


def add(first, second):
    return (first.astype(jnp.float32) + second.astype(jnp.float32)).astype(jnp.bfloat16)


def per_device(
    frames,
    norm_gain,
    router,
    w_in,
    w_out,
    routing,
    head_gain,
    head_weight,
    frame_lengths,
    labels,
    label_lengths,
):
    sections = lax.axis_size("section")
    section_id = lax.axis_index("section")
    group_size = lax.axis_size("expert")
    member = lax.axis_index("expert")
    outer_size = lax.axis_size("dpo")
    inner_size = lax.axis_size("dpi")
    core = lax.axis_index("dpi")
    micro, utt_dev, frame_count, width = frames.shape
    label_max = labels.shape[2]
    experts = w_in.shape[1] * group_size
    hidden = w_in.shape[3]
    pair_count = micro * utt_dev
    per_section = pair_count // sections
    first_pair = section_id * per_section
    group_count = 2 if per_section % (2 * utt_dev) == 0 else 1
    group_pairs = per_section // group_count
    share = (utt_dev * frame_count * 9 + 8 * experts - 1) // (8 * experts)
    capacity = round_up(share * -(-group_pairs // utt_dev), 16)
    span = group_pairs * frame_count
    member_ref = member.astype(jnp.int32).reshape(1)

    def mine_of(value):
        return lax.dynamic_slice_in_dim(value, first_pair, per_section, 0)

    own_ids = routing.reshape(pair_count, frame_count)
    own_table = jnp.concatenate(
        [
            norm_gain,
            jnp.zeros((7, width), jnp.float32),
            jnp.transpose(router[0]).astype(jnp.float32),
            jnp.zeros((round_up(experts, 8) - experts, width), jnp.float32),
        ],
        axis=0,
    )
    own = (w_in[0, 0], w_out[0, 0])
    paired = sections == 2 and inner_size == 2
    if paired:
        other_ids = swap(own_ids, "section")
        other_table = swap(own_table, "section")
        half = hidden // 2
        sent_in = lax.dynamic_slice(own[0], (0, core * half), (width, half))
        sent_out = lax.dynamic_slice(own[1], (core * half, 0), (half, width))
        sent_in, sent_out, other_ids, other_table = lax.optimization_barrier(
            (sent_in, sent_out, other_ids, other_table)
        )
        came_in = swap(sent_in, "section")
        came_out = swap(sent_out, "section")
        other = [(came_in, came_out), (swap(came_in, "dpi"), swap(came_out, "dpi"))]
    else:
        all_ids = lax.all_gather(own_ids, "section")
        all_tables = lax.all_gather(own_table, "section")
        all_in = lax.all_gather(own[0], "section")
        all_out = lax.all_gather(own[1], "section")

    def of_layer(layer):
        if not paired:
            chosen = (all_in[layer], all_out[layer])
            return all_ids[layer], all_tables[layer], chosen, [], jnp.ones((1,), jnp.int32)
        mine = section_id == layer
        return (
            jnp.where(mine, own_ids, other_ids),
            jnp.where(mine, own_table, other_table),
            own,
            other,
            mine.astype(jnp.int32).reshape(1),
        )

    layers = []
    for layer in range(sections):
        ids, table, weights, others, pick_own = of_layer(layer)
        ids = jnp.pad(mine_of(ids), ((0, 0), (0, LANES - frame_count)), constant_values=-1)
        parts = [ids[g * group_pairs : (g + 1) * group_pairs] for g in range(group_count)]
        layers.append((parts, table, weights, others, pick_own))

    rows = lax.dynamic_slice_in_dim(
        frames.reshape(pair_count * frame_count, width),
        first_pair * frame_count,
        per_section * frame_count,
        0,
    )
    current = [rows[g * span : (g + 1) * span] for g in range(group_count)]

    def exchange(blocks, sign):
        return [blocks[0]] + [
            rotate(blocks[k], "expert", sign * k) for k in range(1, group_size)
        ]

    outgoing = [
        dispatch(current[g], layers[0][0][g], member_ref, experts, capacity, frame_count)
        for g in range(group_count)
    ]
    received = [exchange(blocks, 1) for blocks in outgoing]

    notes = jnp.concatenate(
        [
            mine_of(labels.reshape(pair_count, label_max)),
            mine_of(frame_lengths.reshape(pair_count, 1)),
            mine_of(label_lengths.reshape(pair_count, 1)),
        ],
        axis=1,
    )
    if group_size == 4:
        found = [notes] + [rotate(notes, "expert", -k) for k in range(1, group_size)]
        low = member < 2
        notes_all = jnp.stack(
            [
                found[0],
                jnp.where(low, found[1], found[3]),
                found[2],
                jnp.where(low, found[3], found[1]),
            ]
        )
    else:
        notes_all = lax.all_gather(notes, "expert")
    shard = head_weight.shape[1]
    weight_rows = jnp.transpose(head_weight)
    known, all_places = [], []
    for g in range(group_count):
        part = notes_all[:, g * group_pairs : (g + 1) * group_pairs].reshape(
            group_size * group_pairs, label_max + 2
        )
        utterances = part.shape[0]
        names = part[:, :label_max]
        named = jnp.concatenate(
            [
                names,
                jnp.zeros((utterances, 1), jnp.int32),
                jnp.full((utterances, COLS - label_max - 1), -1, jnp.int32),
            ],
            axis=1,
        ).reshape(utterances * COLS)
        local = named - member * shard
        places = jnp.where((named >= 0) & (local >= 0) & (local < shard), local, -1)
        all_places.append(places)
        known.append(
            (
                jnp.pad(names, ((0, 0), (0, LANES - label_max))),
                part[:, label_max : label_max + 1],
                part[:, label_max + 1 :],
                places.reshape(1, -1),
            )
        )
    label_weight = label_rows(weight_rows, jnp.concatenate(all_places).reshape(-1, 1))
    entries = all_places[0].shape[0]
    received, label_weight = lax.optimization_barrier((received, label_weight))

    spread = []
    for layer in range(sections):
        ids, table, weights, others, pick_own = layers[layer]
        for g in range(group_count):
            done = run_expert(received[g], table, weights, others, pick_own)
            returned = exchange(done, -1)
            if layer < sections - 1:
                current[g], blocks = combine_and_dispatch(
                    current[g],
                    returned,
                    ids[g],
                    table,
                    layers[layer + 1][0][g],
                    member_ref,
                    experts,
                    capacity,
                    frame_count,
                )
                received[g] = exchange(blocks, 1)
            else:
                normed = combine_and_norm(
                    current[g],
                    returned,
                    ids[g],
                    table,
                    head_gain.reshape(1, width),
                    member_ref,
                    experts,
                    capacity,
                    frame_count,
                )
                if group_size == 4:
                    spread.append(spread_rows(normed, member))
                else:
                    gathered = lax.all_gather(normed, "expert")
                    spread.append([gathered[k] for k in range(group_size)])

    tables = jnp.asarray(slot_tables(group_size))
    slots = lax.dynamic_index_in_dim(tables, member, 0, keepdims=False)
    groups, my_losses = [], []
    for g in range(group_count):
        logits, rows_all, stats = head_logits(
            spread[g], weight_rows, label_weight[g * entries : (g + 1) * entries], frame_count
        )
        if group_size == 4:
            found = [stats] + [rotate(stats, "expert", -k) for k in range(1, group_size)]
        else:
            gathered = lax.all_gather(stats, "expert")
            found = [
                lax.dynamic_index_in_dim(gathered, (member + k) % group_size, 0, keepdims=False)
                for k in range(group_size)
            ]
        names, frames_all, counts_all, places = known[g]
        out, high, low, losses = ctc_pass(
            found, slots, names, frames_all, counts_all, frame_count, label_max
        )
        own_slot = 0 if group_size == 4 else member
        my_losses.append(
            lax.dynamic_slice(losses, (own_slot * group_pairs, 0), (group_pairs, 1))
        )
        groups.append(
            dict(logits=logits, rows=rows_all, out=out, high=high, low=low, places=places)
        )
    my_losses = jnp.concatenate(my_losses, axis=0)
    blocks = groups[0]["logits"].shape[0] // BLOCK_ROWS
    if paired and outer_size == 2 and blocks == 8:
        outer = lax.axis_index("dpo")

        def pair_of(side, first, second):
            return jnp.stack([side * 4 + first, side * 4 + 2 + second]).astype(jnp.int32)

        sibling_sent = head_gradient(groups, pair_of(1 - core, 1 - section_id, 1 - outer), 2)
        sibling_kept = head_gradient(groups, pair_of(1 - core, section_id, outer), 2)
        came_sent = swap(sibling_sent, "dpi")
        came_kept = swap(sibling_kept, "dpi")
        sent = add(head_gradient(groups, pair_of(core, 1 - section_id, 1 - outer), 2), came_sent)
        first_in = swap(sent[:BLOCK_ROWS], "section")
        second_in = swap(sent[BLOCK_ROWS:], "dpo")
        kept = add(head_gradient(groups, pair_of(core, section_id, outer), 2), came_kept)
        first = add(kept[:BLOCK_ROWS], first_in)
        second = add(kept[BLOCK_ROWS:], second_in)
        part = BLOCK_ROWS // 2

        def piece(value, index):
            return lax.dynamic_slice_in_dim(value, index * part, part, 0)

        first_far = swap(piece(first, 1 - outer), "dpo")
        second_far = swap(piece(second, 1 - section_id), "section")
        final = jnp.concatenate(
            [add(piece(first, outer), first_far), add(piece(second, section_id), second_far)],
            axis=0,
        )
        across = swap(final, "section")
        beside = swap(final, "dpo")
        first_diagonal = swap(beside[:part], "section")
        second_diagonal = swap(across[part:], "dpo")
        mine = [final, across, beside, first_diagonal, second_diagonal]
        theirs = [swap(value, "dpi") for value in mine]
        pieces, offsets = [], []
        for side, held in ((core, mine), (1 - core, theirs)):
            where = (
                (section_id, outer),
                (1 - section_id, outer),
                (section_id, 1 - outer),
            )
            for value, (s, y) in zip(held[:3], where):
                pieces += [value[:part], value[part:]]
                offsets += [
                    side * 1024 + s * 256 + y * 128,
                    side * 1024 + 512 + y * 256 + s * 128,
                ]
            pieces += held[3:]
            s, y = 1 - section_id, 1 - outer
            offsets += [
                side * 1024 + s * 256 + y * 128,
                side * 1024 + 512 + y * 256 + s * 128,
            ]
        whole = assemble(pieces, jnp.stack(offsets).astype(jnp.int32), shard)
    else:
        partial = head_gradient(groups, jnp.arange(blocks, dtype=jnp.int32), blocks)[:shard]
        whole = lax.psum(partial.astype(jnp.float32), ("section", "dpo", "dpi")).astype(
            jnp.bfloat16
        )
    return (my_losses, jnp.transpose(whole))


def solution(mesh):
    sections, group_size, spread = (mesh.shape[name] for name in ("section", "expert", "dp"))
    inner = 2 if spread % 2 == 0 else 1
    split = Mesh(
        mesh.devices.reshape(sections, group_size, spread // inner, inner),
        ("section", "expert", "dpo", "dpi"),
    )
    block = ("expert", "dpo", "dpi")
    placed = (
        P(None, block, None, None),
        P("section", None),
        P("section", None, None),
        P("section", "expert", None, None),
        P("section", "expert", None, None),
        P("section", None, block, None, None),
        P(),
        P(None, "expert"),
        P(None, block),
        P(None, block, None),
        P(None, block),
    )
    return jax.shard_map(
        per_device,
        mesh=split,
        in_specs=placed,
        out_specs=(P("section", block), P(None, "expert")),
        check_vma=False,
    )
```

profile of v0, /device:TPU:0, one launch (start us, length us, event | category | flops | bytes accessed | tf_op | source)
XLA Modules:
  0.0 239.8 jit_solution(11021242545399122510)
XLA Ops:
  2.6 5.1 %collective-permute-start = (s32[4,14]{1,0:T(4,128)S(1)}, s32[4,14]{1,0:T(4,128)S(1)}, u32[]{:S(2)}, u32[]{:S(2)}) collective-permute-start(s32[4,14]{1,0:T(4,128)S(1)} %pad_add_fusion.1), channel_id=1, source_target_pairs={{0,12},{4,0},{8,4},{12,8},{1,13},{5,1},{9,5},{13,9},{2,14},{6,2},{... | collective-permute-start | bytes 680 | tf_op jit(solution)/shard_map/ppermute | solution.py:657
  19.0 3.4 %collective-permute-start.5 = (bf16[32,1280]{1,0:T(8,128)(2,1)S(1)}, bf16[32,1280]{1,0:T(8,128)(2,1)S(1)}, u32[]{:S(2)}, u32[]{:S(2)}) collective-permute-start(bf16[32,1280]{1,0:T(8,128)(2,1)S(1)} %get-tuple-element.65), channel_id=1, source_target_pairs={{0,4},{4,8},{8,12},{12,0},{1,5},{5,9},{9,13},{13,1},{2,6},{6,10},{... | collective-permute-start | bytes 245768 | tf_op jit(solution)/shard_map/ppermute | solution.py:657
  24.9 2.4 %copy-done.9 = bf16[1280,2000]{0,1:T(8,128)(2,1)S(1)} copy-done((bf16[1280,2000]{0,1:T(8,128)(2,1)S(1)}, bf16[1280,2000]{0,1:T(8,128)(2,1)}, u32[]{:S(2)}) %copy-start.9) | copy-done | bytes 5120024
  27.3 4.1 %shard_map.133 = bf16[256,1280]{1,0:T(8,128)(2,1)S(1)} custom-call(s32[256,1]{1,0:T(8,128)S(1)} %copy.29.places_ref, bf16[2000,1280]{1,0:T(8,128)(2,1)S(1)} %bitcast.67), custom_call_target="tpu_custom_call" | custom-call | flops 1342177280 | bytes 6291456 | tf_op jit(solution)/shard_map/pallas_call | solution.py:274
  32.3 2.5 %collective-permute-start.9 = (bf16[32,1280]{1,0:T(8,128)(2,1)S(1)}, bf16[32,1280]{1,0:T(8,128)(2,1)S(1)}, u32[]{:S(2)}, u32[]{:S(2)}) collective-permute-start(bf16[32,1280]{1,0:T(8,128)(2,1)S(1)} %get-tuple-element.70), channel_id=1, source_target_pairs={{0,8},{4,12},{8,0},{12,4},{1,9},{5,13},{9,1},{13,5},{2,10},{6,14},... | collective-permute-start | bytes 245768 | tf_op jit(solution)/shard_map/ppermute | solution.py:657
  40.1 3.4 %collective-permute-start.32 = (bf16[32,1280]{1,0:T(8,128)(2,1)S(1)}, bf16[32,1280]{1,0:T(8,128)(2,1)S(1)}, u32[]{:S(2)}, u32[]{:S(2)}) collective-permute-start(bf16[32,1280]{1,0:T(8,128)(2,1)S(1)} %get-tuple-element.100), channel_id=1, source_target_pairs={{0,12},{4,0},{8,4},{12,8},{1,13},{5,1},{9,5},{13,9},{2,14},{6,2},{... | collective-permute-start | bytes 245768 | tf_op jit(solution)/shard_map/ppermute | solution.py:657
  45.4 3.3 %collective-permute-start.15 = (bf16[32,1280]{1,0:T(8,128)(2,1)S(1)}, bf16[32,1280]{1,0:T(8,128)(2,1)S(1)}, u32[]{:S(2)}, u32[]{:S(2)}) collective-permute-start(bf16[32,1280]{1,0:T(8,128)(2,1)S(1)} %get-tuple-element.81), channel_id=1, source_target_pairs={{0,12},{4,0},{8,4},{12,8},{1,13},{5,1},{9,5},{13,9},{2,14},{6,2},{... | collective-permute-start | bytes 245768 | tf_op jit(solution)/shard_map/ppermute | solution.py:657
  49.9 6.3 %collective-permute-done.33.refs_2_ = bf16[32,1280]{1,0:T(8,128)(2,1)S(1)} collective-permute-done((bf16[32,1280]{1,0:T(8,128)(2,1)S(1)}, bf16[32,1280]{1,0:T(8,128)(2,1)S(1)}, u32[]{:S(2)}, u32[]{:S(2)}) %collective-permute-start.33) | collective-permute-done | bytes 81952 | tf_op jit(solution)/shard_map/ppermute | solution.py:657
  58.7 2.8 %collective-permute-start.37 = (bf16[32,1280]{1,0:T(8,128)(2,1)S(1)}, bf16[32,1280]{1,0:T(8,128)(2,1)S(1)}, u32[]{:S(2)}, u32[]{:S(2)}) collective-permute-start(bf16[32,1280]{1,0:T(8,128)(2,1)S(1)} %get-tuple-element.107), channel_id=1, source_target_pairs={{0,12},{4,0},{8,4},{12,8},{1,13},{5,1},{9,5},{13,9},{2,14},{6,2},{... | collective-permute-start | bytes 245768 | tf_op jit(solution)/shard_map/ppermute | solution.py:657
  64.7 2.9 %collective-permute-start.20 = (bf16[32,1280]{1,0:T(8,128)(2,1)S(1)}, bf16[32,1280]{1,0:T(8,128)(2,1)S(1)}, u32[]{:S(2)}, u32[]{:S(2)}) collective-permute-start(bf16[32,1280]{1,0:T(8,128)(2,1)S(1)} %get-tuple-element.88), channel_id=1, source_target_pairs={{0,12},{4,0},{8,4},{12,8},{1,13},{5,1},{9,5},{13,9},{2,14},{6,2},{... | collective-permute-start | bytes 245768 | tf_op jit(solution)/shard_map/ppermute | solution.py:657
  68.4 5.2 %collective-permute-start.38 = (bf16[32,1280]{1,0:T(8,128)(2,1)S(1)}, bf16[32,1280]{1,0:T(8,128)(2,1)S(1)}, u32[]{:S(2)}, u32[]{:S(2)}) collective-permute-start(bf16[32,1280]{1,0:T(8,128)(2,1)S(1)} %get-tuple-element.109), channel_id=1, source_target_pairs={{0,12},{4,0},{8,4},{12,8},{1,13},{5,1},{9,5},{13,9},{2,14},{6,2},{... | collective-permute-start | bytes 245768 | tf_op jit(solution)/shard_map/ppermute | solution.py:657
  75.1 3.2 %collective-permute-start.21 = (bf16[32,1280]{1,0:T(8,128)(2,1)S(1)}, bf16[32,1280]{1,0:T(8,128)(2,1)S(1)}, u32[]{:S(2)}, u32[]{:S(2)}) collective-permute-start(bf16[32,1280]{1,0:T(8,128)(2,1)S(1)} %get-tuple-element.90), channel_id=1, source_target_pairs={{0,12},{4,0},{8,4},{12,8},{1,13},{5,1},{9,5},{13,9},{2,14},{6,2},{... | collective-permute-start | bytes 245768 | tf_op jit(solution)/shard_map/ppermute | solution.py:657
  79.5 3.2 %collective-permute-done.39.refs_2_ = bf16[32,1280]{1,0:T(8,128)(2,1)S(1)} collective-permute-done((bf16[32,1280]{1,0:T(8,128)(2,1)S(1)}, bf16[32,1280]{1,0:T(8,128)(2,1)S(1)}, u32[]{:S(2)}, u32[]{:S(2)}) %collective-permute-start.39) | collective-permute-done | bytes 81952 | tf_op jit(solution)/shard_map/ppermute | solution.py:657
  84.7 4.6 %collective-permute-start.42 = (bf16[96,1280]{1,0:T(8,128)(2,1)S(1)}, bf16[96,1280]{1,0:T(8,128)(2,1)S(1)}, u32[]{:S(2)}, u32[]{:S(2)}) collective-permute-start(bf16[96,1280]{1,0:T(8,128)(2,1)S(1)} %shard_map.143.refs_0_), channel_id=1, source_target_pairs={{0,4},{4,8},{8,12},{1,5},{5,9},{9,13},{2,6},{6,10},{10,14},{3,7},{... | collective-permute-start | bytes 737288 | tf_op jit(solution)/shard_map/ppermute | solution.py:662
  92.4 4.6 %collective-permute-start.25 = (bf16[96,1280]{1,0:T(8,128)(2,1)S(1)}, bf16[96,1280]{1,0:T(8,128)(2,1)S(1)}, u32[]{:S(2)}, u32[]{:S(2)}) collective-permute-start(bf16[96,1280]{1,0:T(8,128)(2,1)S(1)} %shard_map.137.refs_0_), channel_id=1, source_target_pairs={{0,4},{4,8},{8,12},{1,5},{5,9},{9,13},{2,6},{6,10},{10,14},{3,7},{... | collective-permute-start | bytes 737288 | tf_op jit(solution)/shard_map/ppermute | solution.py:662
  102.7 4.2 %collective-permute-done.43 = bf16[96,1280]{1,0:T(8,128)(2,1)S(1)} collective-permute-done((bf16[96,1280]{1,0:T(8,128)(2,1)S(1)}, bf16[96,1280]{1,0:T(8,128)(2,1)S(1)}, u32[]{:S(2)}, u32[]{:S(2)}) %collective-permute-start.43) | collective-permute-done | bytes 245792 | tf_op jit(solution)/shard_map/ppermute | solution.py:663
  108.3 4.7 %collective-permute-done.26 = bf16[96,1280]{1,0:T(8,128)(2,1)S(1)} collective-permute-done((bf16[96,1280]{1,0:T(8,128)(2,1)S(1)}, bf16[96,1280]{1,0:T(8,128)(2,1)S(1)}, u32[]{:S(2)}, u32[]{:S(2)}) %collective-permute-start.26) | collective-permute-done | bytes 245792 | tf_op jit(solution)/shard_map/ppermute | solution.py:663
  118.3 5.7 %shard_map.144 = (f32[2048,384]{1,0:T(8,128)S(1)}, bf16[384,1280]{1,0:T(8,128)(2,1)S(1)}, f32[4,16,96]{2,1,0:T(8,128)S(1)}) custom-call(bf16[2000,1280]{1,0:T(8,128)(2,1)S(1)} %bitcast.68, bf16[128,1280]{1,0:T(8,128)(2,1)S(1)} %get-tuple-element.145.label_ref, bf16[96,1280]{1,0:T(8,128)(2,1)S(1)} %copy-done.21, ...), custom_call_target="tpu_custom_call" | custom-call | flops 2013265920 | bytes 9437184 | tf_op jit(solution)/shard_map/pallas_call | solution.py:343
  124.0 5.4 %collective-permute-start.46 = (f32[4,16,96]{2,1,0:T(8,128)S(1)}, f32[4,16,96]{2,1,0:T(8,128)S(1)}, u32[]{:S(2)}, u32[]{:S(2)}) collective-permute-start(f32[4,16,96]{2,1,0:T(8,128)S(1)} %get-tuple-element.112.refs_0_), channel_id=1, source_target_pairs={{0,12},{4,0},{8,4},{12,8},{1,13},{5,1},{9,5},{13,9},{2,14},{6,2},{... | collective-permute-start | bytes 73736 | tf_op jit(solution)/shard_map/ppermute | solution.py:657
  131.2 5.7 %shard_map.138 = (f32[2048,384]{1,0:T(8,128)S(1)}, bf16[384,1280]{1,0:T(8,128)(2,1)S(1)}, f32[4,16,96]{2,1,0:T(8,128)S(1)}) custom-call(bf16[2000,1280]{1,0:T(8,128)(2,1)S(1)} %bitcast.69, bf16[128,1280]{1,0:T(8,128)(2,1)S(1)} %get-tuple-element.144.label_ref, bf16[96,1280]{1,0:T(8,128)(2,1)S(1)} %shard_map.137.refs_0_, ...), custom_call_target="tpu_custom_call" | custom-call | flops 2013265920 | bytes 9437184 | tf_op jit(solution)/shard_map/pallas_call | solution.py:343
  140.3 10.8 %shard_map.145 = (f32[16,384]{1,0:T(8,128)S(1)}, bf16[128,384]{1,0:T(8,128)(2,1)S(1)}, bf16[128,384]{1,0:T(8,128)(2,1)S(1)}, f32[8,128]{1,0:T(8,128)S(1)}) custom-call(s32[16]{0:T(128)S(1)} %fusion.4.slots_ref, s32[8,128]{1,0:T(8,128)S(1)} %pad.17.labels_ref, s32[8,1]{1,0:T(8,128)S(1)} %get-tuple-element.159.frames_ref, ...), custom_call_target="tpu_custom_call" | custom-call | flops 67108864 | bytes 1048576 | tf_op jit(solution)/shard_map/pallas_call | solution.py:520
  151.8 10.8 %shard_map.139 = (f32[16,384]{1,0:T(8,128)S(1)}, bf16[128,384]{1,0:T(8,128)(2,1)S(1)}, bf16[128,384]{1,0:T(8,128)(2,1)S(1)}, f32[8,128]{1,0:T(8,128)S(1)}) custom-call(s32[16]{0:T(128)S(1)} %copy-done.23, s32[8,128]{1,0:T(8,128)S(1)} %pad.14.labels_ref, s32[8,1]{1,0:T(8,128)S(1)} %copy-done.15, s32[8,1]{1,0:T(8,128)S(1)} %get-tuple-element.156.counts_ref, ...), custom_call_target="tpu_custom_call" | custom-call | flops 67108864 | bytes 1048576 | tf_op jit(solution)/shard_map/pallas_call | solution.py:520
  162.7 3.7 %shard_map.149 = bf16[512,1280]{1,0:T(8,128)(2,1)} custom-call(s32[2]{0:T(128)S(1)} %copy-done.17, f32[2048,384]{1,0:T(8,128)S(1)} %get-tuple-element.114.refs_0_, bf16[384,1280]{1,0:T(8,128)(2,1)S(1)} %get-tuple-element.115.refs_1_, f32[16,384]{1,0:T(8,128)S(1)} %get-tuple-element.116.refs_2_, bf16[128,384]{1,0:T(8,128)(2,1)S(1)} %get-tuple-element.117.refs_3_, ...), custom_call_target="tpu_custom_call" | custom-call | flops 1207959552 | bytes 10485760 | tf_op jit(solution)/shard_map/pallas_call | solution.py:590
  172.4 2.8 %shard_map.147 = bf16[512,1280]{1,0:T(8,128)(2,1)S(1)} custom-call(s32[2]{0:T(128)S(1)} %copy-done.16, f32[2048,384]{1,0:T(8,128)S(1)} %copy-done.2, bf16[384,1280]{1,0:T(8,128)(2,1)S(1)} %copy-done.6, f32[16,384]{1,0:T(8,128)S(1)} %copy-done.14, bf16[128,384]{1,0:T(8,128)(2,1)S(1)} %get-tuple-element.117.refs_3_, ...), custom_call_target="tpu_custom_call" | custom-call | flops 1207959552 | bytes 10485760 | tf_op jit(solution)/shard_map/pallas_call | solution.py:590
  175.8 2.8 %shard_map.148 = bf16[512,1280]{1,0:T(8,128)(2,1)S(1)} custom-call(s32[2]{0:T(128)S(1)} %pad_add_fusion.5.order_ref, f32[2048,384]{1,0:T(8,128)S(1)} %copy-done.2, bf16[384,1280]{1,0:T(8,128)(2,1)S(1)} %copy-done.6, f32[16,384]{1,0:T(8,128)S(1)} %copy-done.14, bf16[128,384]{1,0:T(8,128)(2,1)S(1)} %get-tuple-element.117.refs_3_, ...), custom_call_target="tpu_custom_call" | custom-call | flops 1207959552 | bytes 10485760 | tf_op jit(solution)/shard_map/pallas_call | solution.py:590
  182.8 2.8 %shard_map.146 = bf16[512,1280]{1,0:T(8,128)(2,1)S(1)} custom-call(s32[2]{0:T(128)S(1)} %pad_add_fusion.3.order_ref, f32[2048,384]{1,0:T(8,128)S(1)} %copy-done.2, bf16[384,1280]{1,0:T(8,128)(2,1)S(1)} %copy-done.6, f32[16,384]{1,0:T(8,128)S(1)} %copy-done.14, bf16[128,384]{1,0:T(8,128)(2,1)S(1)} %get-tuple-element.117.refs_3_, ...), custom_call_target="tpu_custom_call" | custom-call | flops 1207959552 | bytes 10485760 | tf_op jit(solution)/shard_map/pallas_call | solution.py:590
  186.0 11.1 %collective-permute-done.53 = bf16[256,1280]{1,0:T(8,128)(2,1)S(1)} collective-permute-done((bf16[256,1280]{1,0:T(8,128)(2,1)S(1)}, bf16[256,1280]{1,0:T(8,128)(2,1)S(1)}, u32[]{:S(2)}, u32[]{:S(2)}) %collective-permute-start.53) | collective-permute-done | bytes 655392 | tf_op jit(solution)/shard_map/ppermute | solution.py:652
  200.5 6.9 %collective-permute-done.52 = bf16[128,1280]{1,0:T(8,128)(2,1)S(1)} collective-permute-done((bf16[128,1280]{1,0:T(8,128)(2,1)S(1)}, bf16[128,1280]{1,0:T(8,128)(2,1)S(1)}, u32[]{:S(2)}, u32[]{:S(2)}) %collective-permute-start.52) | collective-permute-done | bytes 327712 | tf_op jit(solution)/shard_map/ppermute | solution.py:652
  212.4 9.9 %collective-permute-done.56 = bf16[256,1280]{1,0:T(8,128)(2,1)S(1)} collective-permute-done((bf16[256,1280]{1,0:T(8,128)(2,1)S(1)}, bf16[256,1280]{1,0:T(8,128)(2,1)S(1)}, u32[]{:S(2)}, u32[]{:S(2)}) %collective-permute-start.56) | collective-permute-done | bytes 655392 | tf_op jit(solution)/shard_map/ppermute | solution.py:652
  225.6 4.8 %collective-permute-done.57.refs_6_ = bf16[128,1280]{1,0:T(8,128)(2,1)S(1)} collective-permute-done((bf16[128,1280]{1,0:T(8,128)(2,1)S(1)}, bf16[128,1280]{1,0:T(8,128)(2,1)S(1)}, u32[]{:S(2)}, u32[]{:S(2)}) %collective-permute-start.57) | collective-permute-done | bytes 327712 | tf_op jit(solution)/shard_map/ppermute | solution.py:652
  230.5 4.6 %collective-permute-done.58.refs_7_ = bf16[128,1280]{1,0:T(8,128)(2,1)S(1)} collective-permute-done((bf16[128,1280]{1,0:T(8,128)(2,1)S(1)}, bf16[128,1280]{1,0:T(8,128)(2,1)S(1)}, u32[]{:S(2)}, u32[]{:S(2)}) %collective-permute-start.58) | collective-permute-done | bytes 327712 | tf_op jit(solution)/shard_map/ppermute | solution.py:652
  236.7 3.0 %shard_map.150 = bf16[2000,1280]{1,0:T(8,128)(2,1)} custom-call(s32[16]{0:T(128)S(1)} %stack.123.offsets_ref, bf16[128,1280]{1,0:T(8,128)(2,1)S(1)} %add_convert_fusion.5.refs_0_, bf16[128,1280]{1,0:T(8,128)(2,1)S(1)} %add_convert_fusion.4.refs_1_, bf16[128,1280]{1,0:T(8,128)(2,1)S(1)} %get-tuple-element.143.refs_2_, ...), custom_call_target="tpu_custom_call" | custom-call | bytes 10240000 | tf_op jit(solution)/shard_map/pallas_call | solution.py:640
  (249 shorter events, 81.2 us)
Async XLA Ops:
  2.6 12.1 %collective-permute-start = (s32[4,14]{1,0:T(4,128)S(1)}, s32[4,14]{1,0:T(4,128)S(1)}, u32[]{:S(2)}, u32[]{:S(2)}) collective-permute-start(s32[4,14]{1,0:T(4,128)S(1)} %pad_add_fusion.1), channel_id=1, source_target_pairs={{0,12},{4,0},{8,4},{12,8},{1,13},{5,1},{9,5},{13,9},{2,14},{6,2},{... | collective-permute-start | bytes 680 | tf_op jit(solution)/shard_map/ppermute | solution.py:657
  16.3 19.9 %collective-permute-start.11 = (bf16[1280,128]{1,0:T(8,128)(2,1)S(1)}, bf16[1280,128]{1,0:T(8,128)(2,1)S(1)}, u32[]{:S(2)}, u32[]{:S(2)}) collective-permute-start(bf16[1280,128]{1,0:T(8,128)(2,1)S(1)} %dynamic-slice_bitcast_fusion.1), channel_id=1, source_target_pairs={{0,16},{16,0},{1,17},{17,1},{2,18},{18,2},{3,19},{19,3},{4,20},{20... | collective-permute-start | bytes 983048 | tf_op jit(solution)/shard_map/ppermute | solution.py:652
  16.9 19.2 %collective-permute-start.12 = (bf16[128,1280]{1,0:T(8,128)(2,1)S(1)}, bf16[128,1280]{1,0:T(8,128)(2,1)S(1)}, u32[]{:S(2)}, u32[]{:S(2)}) collective-permute-start(bf16[128,1280]{1,0:T(8,128)(2,1)S(1)} %dynamic-slice_bitcast_fusion), channel_id=1, source_target_pairs={{0,16},{16,0},{1,17},{17,1},{2,18},{18,2},{3,19},{19,3},{4,20},{20... | collective-permute-start | bytes 983048 | tf_op jit(solution)/shard_map/ppermute | solution.py:652
  19.0 13.1 %collective-permute-start.5 = (bf16[32,1280]{1,0:T(8,128)(2,1)S(1)}, bf16[32,1280]{1,0:T(8,128)(2,1)S(1)}, u32[]{:S(2)}, u32[]{:S(2)}) collective-permute-start(bf16[32,1280]{1,0:T(8,128)(2,1)S(1)} %get-tuple-element.65), channel_id=1, source_target_pairs={{0,4},{4,8},{8,12},{12,0},{1,5},{5,9},{9,13},{13,1},{2,6},{6,10},{... | collective-permute-start | bytes 245768 | tf_op jit(solution)/shard_map/ppermute | solution.py:657
  22.4 12.3 %collective-permute-start.7 = (bf16[32,1280]{1,0:T(8,128)(2,1)S(1)}, bf16[32,1280]{1,0:T(8,128)(2,1)S(1)}, u32[]{:S(2)}, u32[]{:S(2)}) collective-permute-start(bf16[32,1280]{1,0:T(8,128)(2,1)S(1)} %get-tuple-element.67), channel_id=1, source_target_pairs={{0,12},{4,0},{8,4},{12,8},{1,13},{5,1},{9,5},{13,9},{2,14},{6,2},{... | collective-permute-start | bytes 245768 | tf_op jit(solution)/shard_map/ppermute | solution.py:657
  44.1 12.0 %collective-permute-start.33 = (bf16[32,1280]{1,0:T(8,128)(2,1)S(1)}, bf16[32,1280]{1,0:T(8,128)(2,1)S(1)}, u32[]{:S(2)}, u32[]{:S(2)}) collective-permute-start(bf16[32,1280]{1,0:T(8,128)(2,1)S(1)} %get-tuple-element.101), channel_id=1, source_target_pairs={{0,8},{4,12},{8,0},{12,4},{1,9},{5,13},{9,1},{13,5},{2,10},{6,14},... | collective-permute-start | bytes 245768 | tf_op jit(solution)/shard_map/ppermute | solution.py:657
  44.2 12.0 %collective-permute-start.34 = (bf16[32,1280]{1,0:T(8,128)(2,1)S(1)}, bf16[32,1280]{1,0:T(8,128)(2,1)S(1)}, u32[]{:S(2)}, u32[]{:S(2)}) collective-permute-start(bf16[32,1280]{1,0:T(8,128)(2,1)S(1)} %get-tuple-element.102), channel_id=1, source_target_pairs={{0,4},{4,8},{8,12},{12,0},{1,5},{5,9},{9,13},{13,1},{2,6},{6,10},{... | collective-permute-start | bytes 245768 | tf_op jit(solution)/shard_map/ppermute | solution.py:657
  45.4 13.2 %collective-permute-start.15 = (bf16[32,1280]{1,0:T(8,128)(2,1)S(1)}, bf16[32,1280]{1,0:T(8,128)(2,1)S(1)}, u32[]{:S(2)}, u32[]{:S(2)}) collective-permute-start(bf16[32,1280]{1,0:T(8,128)(2,1)S(1)} %get-tuple-element.81), channel_id=1, source_target_pairs={{0,12},{4,0},{8,4},{12,8},{1,13},{5,1},{9,5},{13,9},{2,14},{6,2},{... | collective-permute-start | bytes 245768 | tf_op jit(solution)/shard_map/ppermute | solution.py:657
  48.7 12.8 %collective-permute-start.16 = (bf16[32,1280]{1,0:T(8,128)(2,1)S(1)}, bf16[32,1280]{1,0:T(8,128)(2,1)S(1)}, u32[]{:S(2)}, u32[]{:S(2)}) collective-permute-start(bf16[32,1280]{1,0:T(8,128)(2,1)S(1)} %get-tuple-element.82), channel_id=1, source_target_pairs={{0,8},{4,12},{8,0},{12,4},{1,9},{5,13},{9,1},{13,5},{2,10},{6,14},... | collective-permute-start | bytes 245768 | tf_op jit(solution)/shard_map/ppermute | solution.py:657
  49.8 11.7 %collective-permute-start.17 = (bf16[32,1280]{1,0:T(8,128)(2,1)S(1)}, bf16[32,1280]{1,0:T(8,128)(2,1)S(1)}, u32[]{:S(2)}, u32[]{:S(2)}) collective-permute-start(bf16[32,1280]{1,0:T(8,128)(2,1)S(1)} %get-tuple-element.83), channel_id=1, source_target_pairs={{0,4},{4,8},{8,12},{12,0},{1,5},{5,9},{9,13},{13,1},{2,6},{6,10},{... | collective-permute-start | bytes 245768 | tf_op jit(solution)/shard_map/ppermute | solution.py:657
  62.5 11.1 %collective-permute-start.18 = (bf16[32,1280]{1,0:T(8,128)(2,1)S(1)}, bf16[32,1280]{1,0:T(8,128)(2,1)S(1)}, u32[]{:S(2)}, u32[]{:S(2)}) collective-permute-start(bf16[32,1280]{1,0:T(8,128)(2,1)S(1)} %get-tuple-element.86), channel_id=1, source_target_pairs={{0,4},{4,8},{8,12},{12,0},{1,5},{5,9},{9,13},{13,1},{2,6},{6,10},{... | collective-permute-start | bytes 245768 | tf_op jit(solution)/shard_map/ppermute | solution.py:657
  63.2 11.1 %collective-permute-start.19 = (bf16[32,1280]{1,0:T(8,128)(2,1)S(1)}, bf16[32,1280]{1,0:T(8,128)(2,1)S(1)}, u32[]{:S(2)}, u32[]{:S(2)}) collective-permute-start(bf16[32,1280]{1,0:T(8,128)(2,1)S(1)} %get-tuple-element.87), channel_id=1, source_target_pairs={{0,8},{4,12},{8,0},{12,4},{1,9},{5,13},{9,1},{13,5},{2,10},{6,14},... | collective-permute-start | bytes 245768 | tf_op jit(solution)/shard_map/ppermute | solution.py:657
  68.4 11.1 %collective-permute-start.38 = (bf16[32,1280]{1,0:T(8,128)(2,1)S(1)}, bf16[32,1280]{1,0:T(8,128)(2,1)S(1)}, u32[]{:S(2)}, u32[]{:S(2)}) collective-permute-start(bf16[32,1280]{1,0:T(8,128)(2,1)S(1)} %get-tuple-element.109), channel_id=1, source_target_pairs={{0,12},{4,0},{8,4},{12,8},{1,13},{5,1},{9,5},{13,9},{2,14},{6,2},{... | collective-permute-start | bytes 245768 | tf_op jit(solution)/shard_map/ppermute | solution.py:657
  75.1 15.2 %collective-permute-start.21 = (bf16[32,1280]{1,0:T(8,128)(2,1)S(1)}, bf16[32,1280]{1,0:T(8,128)(2,1)S(1)}, u32[]{:S(2)}, u32[]{:S(2)}) collective-permute-start(bf16[32,1280]{1,0:T(8,128)(2,1)S(1)} %get-tuple-element.90), channel_id=1, source_target_pairs={{0,12},{4,0},{8,4},{12,8},{1,13},{5,1},{9,5},{13,9},{2,14},{6,2},{... | collective-permute-start | bytes 245768 | tf_op jit(solution)/shard_map/ppermute | solution.py:657
  78.3 12.0 %collective-permute-start.22 = (bf16[32,1280]{1,0:T(8,128)(2,1)S(1)}, bf16[32,1280]{1,0:T(8,128)(2,1)S(1)}, u32[]{:S(2)}, u32[]{:S(2)}) collective-permute-start(bf16[32,1280]{1,0:T(8,128)(2,1)S(1)} %get-tuple-element.91), channel_id=1, source_target_pairs={{0,8},{4,12},{8,0},{12,4},{1,9},{5,13},{9,1},{13,5},{2,10},{6,14},... | collective-permute-start | bytes 245768 | tf_op jit(solution)/shard_map/ppermute | solution.py:657
  83.4 13.6 %collective-permute-start.41 = (bf16[96,1280]{1,0:T(8,128)(2,1)S(1)}, bf16[96,1280]{1,0:T(8,128)(2,1)S(1)}, u32[]{:S(2)}, u32[]{:S(2)}) collective-permute-start(bf16[96,1280]{1,0:T(8,128)(2,1)S(1)} %shard_map.143.refs_0_), channel_id=1, source_target_pairs={{4,0},{8,4},{12,8},{5,1},{9,5},{13,9},{6,2},{10,6},{14,10},{7,3},{... | collective-permute-start | bytes 737288 | tf_op jit(solution)/shard_map/ppermute | solution.py:661
  84.7 13.6 %collective-permute-start.42 = (bf16[96,1280]{1,0:T(8,128)(2,1)S(1)}, bf16[96,1280]{1,0:T(8,128)(2,1)S(1)}, u32[]{:S(2)}, u32[]{:S(2)}) collective-permute-start(bf16[96,1280]{1,0:T(8,128)(2,1)S(1)} %shard_map.143.refs_0_), channel_id=1, source_target_pairs={{0,4},{4,8},{8,12},{1,5},{5,9},{9,13},{2,6},{6,10},{10,14},{3,7},{... | collective-permute-start | bytes 737288 | tf_op jit(solution)/shard_map/ppermute | solution.py:662
  100.7 12.3 %collective-permute-start.26 = (bf16[96,1280]{1,0:T(8,128)(2,1)S(1)}, bf16[96,1280]{1,0:T(8,128)(2,1)S(1)}, u32[]{:S(2)}, u32[]{:S(2)}) collective-permute-start(bf16[96,1280]{1,0:T(8,128)(2,1)S(1)} %collective-permute-done.24), channel_id=1, source_target_pairs={{4,0},{8,4},{5,1},{9,5},{6,2},{10,6},{7,3},{11,7},{20,16},{24,20},... | collective-permute-start | bytes 737288 | tf_op jit(solution)/shard_map/ppermute | solution.py:663
  102.0 11.0 %collective-permute-start.27 = (bf16[96,1280]{1,0:T(8,128)(2,1)S(1)}, bf16[96,1280]{1,0:T(8,128)(2,1)S(1)}, u32[]{:S(2)}, u32[]{:S(2)}) collective-permute-start(bf16[96,1280]{1,0:T(8,128)(2,1)S(1)} %collective-permute-done.25), channel_id=1, source_target_pairs={{4,8},{8,12},{5,9},{9,13},{6,10},{10,14},{7,11},{11,15},{20,24},{2... | collective-permute-start | bytes 737288 | tf_op jit(solution)/shard_map/ppermute | solution.py:664
  113.0 18.1 %collective-permute-start.28 = (bf16[96,1280]{1,0:T(8,128)(2,1)S(1)}, bf16[96,1280]{1,0:T(8,128)(2,1)S(1)}, u32[]{:S(2)}, u32[]{:S(2)}) collective-permute-start(bf16[96,1280]{1,0:T(8,128)(2,1)S(1)} %broadcast_select_fusion.2.refs_2_), channel_id=1, source_target_pairs={{4,0},{8,12},{5,1},{9,13},{6,2},{10,14},{7,3},{11,15},{20,16},{24,... | collective-permute-start | bytes 737288 | tf_op jit(solution)/shard_map/ppermute | solution.py:668
  124.0 16.2 %collective-permute-start.46 = (f32[4,16,96]{2,1,0:T(8,128)S(1)}, f32[4,16,96]{2,1,0:T(8,128)S(1)}, u32[]{:S(2)}, u32[]{:S(2)}) collective-permute-start(f32[4,16,96]{2,1,0:T(8,128)S(1)} %get-tuple-element.112.refs_0_), channel_id=1, source_target_pairs={{0,12},{4,0},{8,4},{12,8},{1,13},{5,1},{9,5},{13,9},{2,14},{6,2},{... | collective-permute-start | bytes 73736 | tf_op jit(solution)/shard_map/ppermute | solution.py:657
  129.3 10.9 %collective-permute-start.47 = (f32[4,16,96]{2,1,0:T(8,128)S(1)}, f32[4,16,96]{2,1,0:T(8,128)S(1)}, u32[]{:S(2)}, u32[]{:S(2)}) collective-permute-start(f32[4,16,96]{2,1,0:T(8,128)S(1)} %get-tuple-element.112.refs_0_), channel_id=1, source_target_pairs={{0,8},{4,12},{8,0},{12,4},{1,9},{5,13},{9,1},{13,5},{2,10},{6,14},... | collective-permute-start | bytes 73736 | tf_op jit(solution)/shard_map/ppermute | solution.py:657
  129.4 10.9 %collective-permute-start.48 = (f32[4,16,96]{2,1,0:T(8,128)S(1)}, f32[4,16,96]{2,1,0:T(8,128)S(1)}, u32[]{:S(2)}, u32[]{:S(2)}) collective-permute-start(f32[4,16,96]{2,1,0:T(8,128)S(1)} %get-tuple-element.112.refs_0_), channel_id=1, source_target_pairs={{0,4},{4,8},{8,12},{12,0},{1,5},{5,9},{9,13},{13,1},{2,6},{6,10},{... | collective-permute-start | bytes 73736 | tf_op jit(solution)/shard_map/ppermute | solution.py:657
  136.9 14.2 %collective-permute-start.29 = (f32[4,16,96]{2,1,0:T(8,128)S(1)}, f32[4,16,96]{2,1,0:T(8,128)S(1)}, u32[]{:S(2)}, u32[]{:S(2)}) collective-permute-start(f32[4,16,96]{2,1,0:T(8,128)S(1)} %get-tuple-element.93.refs_0_), channel_id=1, source_target_pairs={{0,12},{4,0},{8,4},{12,8},{1,13},{5,1},{9,5},{13,9},{2,14},{6,2},{... | collective-permute-start | bytes 73736 | tf_op jit(solution)/shard_map/ppermute | solution.py:657
  139.1 12.1 %collective-permute-start.30 = (f32[4,16,96]{2,1,0:T(8,128)S(1)}, f32[4,16,96]{2,1,0:T(8,128)S(1)}, u32[]{:S(2)}, u32[]{:S(2)}) collective-permute-start(f32[4,16,96]{2,1,0:T(8,128)S(1)} %get-tuple-element.93.refs_0_), channel_id=1, source_target_pairs={{0,8},{4,12},{8,0},{12,4},{1,9},{5,13},{9,1},{13,5},{2,10},{6,14},... | collective-permute-start | bytes 73736 | tf_op jit(solution)/shard_map/ppermute | solution.py:657
  140.2 10.9 %collective-permute-start.31 = (f32[4,16,96]{2,1,0:T(8,128)S(1)}, f32[4,16,96]{2,1,0:T(8,128)S(1)}, u32[]{:S(2)}, u32[]{:S(2)}) collective-permute-start(f32[4,16,96]{2,1,0:T(8,128)S(1)} %get-tuple-element.93.refs_0_), channel_id=1, source_target_pairs={{0,4},{4,8},{8,12},{12,0},{1,5},{5,9},{9,13},{13,1},{2,6},{6,10},{... | collective-permute-start | bytes 73736 | tf_op jit(solution)/shard_map/ppermute | solution.py:657
  166.4 12.2 %collective-permute-start.50 = (bf16[512,1280]{1,0:T(8,128)(2,1)}, bf16[512,1280]{1,0:T(8,128)(2,1)}, u32[]{:S(2)}, u32[]{:S(2)}) collective-permute-start(bf16[512,1280]{1,0:T(8,128)(2,1)} %shard_map.149), channel_id=1, source_target_pairs={{0,1},{1,0},{2,3},{3,2},{4,5},{5,4},{6,7},{7,6},{8,9},{9,8},{10,11... | collective-permute-start | bytes 3932168 | tf_op jit(solution)/shard_map/ppermute | solution.py:652
  180.4 16.7 %collective-permute-start.53 = (bf16[256,1280]{1,0:T(8,128)(2,1)S(1)}, bf16[256,1280]{1,0:T(8,128)(2,1)S(1)}, u32[]{:S(2)}, u32[]{:S(2)}) collective-permute-start(bf16[256,1280]{1,0:T(8,128)(2,1)S(1)} %get-tuple-element.130), channel_id=1, source_target_pairs={{0,2},{2,0},{1,3},{3,1},{4,6},{6,4},{5,7},{7,5},{8,10},{10,8},{9,1... | collective-permute-start | bytes 1966088 | tf_op jit(solution)/shard_map/ppermute | solution.py:652
  182.0 16.4 %collective-permute-start.51 = (bf16[256,1280]{1,0:T(8,128)(2,1)S(1)}, bf16[256,1280]{1,0:T(8,128)(2,1)S(1)}, u32[]{:S(2)}, u32[]{:S(2)}) collective-permute-start(bf16[256,1280]{1,0:T(8,128)(2,1)S(1)} %get-tuple-element.131), channel_id=1, source_target_pairs={{0,16},{16,0},{1,17},{17,1},{2,18},{18,2},{3,19},{19,3},{4,20},{20... | collective-permute-start | bytes 1966088 | tf_op jit(solution)/shard_map/ppermute | solution.py:652
  207.9 14.5 %collective-permute-start.56 = (bf16[256,1280]{1,0:T(8,128)(2,1)S(1)}, bf16[256,1280]{1,0:T(8,128)(2,1)S(1)}, u32[]{:S(2)}, u32[]{:S(2)}) collective-permute-start(bf16[256,1280]{1,0:T(8,128)(2,1)S(1)} %pad_maximum_fusion), channel_id=1, source_target_pairs={{0,2},{2,0},{1,3},{3,1},{4,6},{6,4},{5,7},{7,5},{8,10},{10,8},{9,1... | collective-permute-start | bytes 1966088 | tf_op jit(solution)/shard_map/ppermute | solution.py:652
  209.4 15.5 %collective-permute-start.55 = (bf16[256,1280]{1,0:T(8,128)(2,1)S(1)}, bf16[256,1280]{1,0:T(8,128)(2,1)S(1)}, u32[]{:S(2)}, u32[]{:S(2)}) collective-permute-start(bf16[256,1280]{1,0:T(8,128)(2,1)S(1)} %pad_maximum_fusion), channel_id=1, source_target_pairs={{0,16},{16,0},{1,17},{17,1},{2,18},{18,2},{3,19},{19,3},{4,20},{20... | collective-permute-start | bytes 1966088 | tf_op jit(solution)/shard_map/ppermute | solution.py:652
  212.4 13.1 %collective-permute-start.59 = (bf16[256,1280]{1,0:T(8,128)(2,1)S(1)}, bf16[256,1280]{1,0:T(8,128)(2,1)S(1)}, u32[]{:S(2)}, u32[]{:S(2)}) collective-permute-start(bf16[256,1280]{1,0:T(8,128)(2,1)S(1)} %pad_maximum_fusion), channel_id=1, source_target_pairs={{0,1},{1,0},{2,3},{3,2},{4,5},{5,4},{6,7},{7,6},{8,9},{9,8},{10,11... | collective-permute-start | bytes 1966088 | tf_op jit(solution)/shard_map/ppermute | solution.py:652
  (60 other events, 630.5 us)
where the time goes:
time: 241 us; the launch traced here: 240 us
  starting transfers between devices  85.2 us (35%)
  waiting for transfers between devices  67 us (28%)
  Pallas kernels  60.1 us (25%)
  local copies, waits for them, and re-layouts  19.8 us (8%)
  other arithmetic  5.89 us (2%)
    ppermute x33, starting transfers between devices, rotate(): lax.ppermute(value, axis, [(i, (i + by) % count) for i in range(count)])  53.7 us
    ppermute x21, waiting for transfers between devices, swap(): return lax.ppermute(value, axis, [(0, 1), (1, 0)])  43 us
    pallas_call x2, Pallas kernels, ctc_pass(): call(kernel, (jax.ShapeDtypeStruct((COLS, row_count), jnp.float32), bf16_...  21.6 us
    ppermute x21, starting transfers between devices, swap(): return lax.ppermute(value, axis, [(0, 1), (1, 0)])  13.1 us
    unnamed x58, local copies, waits for them, and re-layouts  13 us
    pallas_call x4, Pallas kernels, head_gradient(): call(kernel, bf16_rows(blocks * BLOCK_ROWS, width), 2 * blocks * BLOCK_RO...  12.2 us
    ppermute x33, waiting for transfers between devices, rotate(): lax.ppermute(value, axis, [(i, (i + by) % count) for i in range(count)])  12.2 us
    pallas_call x2, Pallas kernels, head_logits(): call(kernel, (jax.ShapeDtypeStruct((blocks * BLOCK_ROWS, row_count), jnp....  11.4 us
  transfers between devices with their start and end apart: 64, of which 18 were waited for; matrix products, arithmetic and copies ran while one was open for 5% of the time, Pallas kernels for 18%

commit v1 on v0

--- a/solution.py
+++ b/solution.py
@@ -9,6 +9,7 @@
 EPSILON = 1e-06
 LOG_ZERO = -1e30
 VMEM_LIMIT = 24 * 1024 * 1024
+STREAM_LIMIT = 58 * 1024 * 1024
 LANES = 128
 COLS = 16
 PEAK, TOTAL, WHOLE = COLS - 3, COLS - 2, COLS - 3
@@ -29,11 +30,11 @@
     return pl.BlockSpec(memory_space=pltpu.SMEM)
 
 
-def call(kernel, out_shape, flops=0, moved=0, **options):
+def call(kernel, out_shape, flops=0, moved=0, limit=VMEM_LIMIT, **options):
     return pl.pallas_call(
         kernel,
         out_shape=out_shape,
-        compiler_params=pltpu.CompilerParams(vmem_limit_bytes=VMEM_LIMIT),
+        compiler_params=pltpu.CompilerParams(vmem_limit_bytes=limit),
         cost_estimate=pl.CostEstimate(flops=flops, bytes_accessed=moved, transcendentals=0),
         **options,
     )
@@ -276,6 +277,7 @@
         bf16_rows(entries, width),
         2 * blocks * BLOCK_ROWS * entries * width,
         6 << 20,
+        STREAM_LIMIT,
         grid=(blocks,),
         in_specs=[
             pl.BlockSpec((entries, 1), lambda i: (0, 0)),
@@ -286,8 +288,10 @@
     )(places, weight)
 
 
-def head_logits(pieces, weight, label_weight, frame_count):
-    count = len(pieces)
+def head_logits(pieces, member, weight, label_weight, frame_count):
+    given = len(pieces)
+    line = given == 5
+    count = 4 if line else given
     span, width = pieces[0].shape
     row_count = count * span
     shard = weight.shape[0]
@@ -295,15 +299,34 @@
     used = shard - (blocks - 1) * BLOCK_ROWS
     entries = label_weight.shape[0]
 
-    def kernel(weight_ref, label_ref, *refs):
-        piece_refs = refs[:count]
-        logits_ref, rows_ref, stats_ref, peak_ref, total_ref = refs[count:]
+    def kernel(member_ref, weight_ref, label_ref, *refs):
+        piece_refs = refs[:given]
+        logits_ref, rows_ref, stats_ref, peak_ref, total_ref = refs[given:]
         step = pl.program_id(0)
 
         @pl.when(step == 0)
         def _():
-            for slot in range(count):
-                rows_ref[slot * span : (slot + 1) * span] = piece_refs[slot][...]
+            def put(slot, piece_ref):
+                rows_ref[slot * span : (slot + 1) * span] = piece_ref[...]
+
+            def put_if(condition, slot, piece_ref):
+                @pl.when(condition)
+                def _():
+                    put(slot, piece_ref)
+
+            if line:
+                value_ref, left_ref, right_ref, far_ref, end_ref = piece_refs
+                place = member_ref[0]
+                put(0, value_ref)
+                put_if(place < 2, 1, left_ref)
+                put_if(place >= 2, 1, right_ref)
+                put(2, far_ref)
+                put_if((place == 0) | (place == 3), 3, end_ref)
+                put_if(place == 1, 3, right_ref)
+                put_if(place == 2, 3, left_ref)
+            else:
+                for slot in range(count):
+                    put(slot, piece_refs[slot])
             peak_ref[...] = jnp.full(peak_ref.shape, LOG_ZERO, jnp.float32)
             total_ref[...] = jnp.zeros(total_ref.shape, jnp.float32)
 
@@ -349,12 +372,14 @@
         ),
         2 * blocks * BLOCK_ROWS * row_count * width,
         9 << 20,
+        STREAM_LIMIT,
         grid=(blocks,),
         in_specs=[
+            smem_spec(),
             pl.BlockSpec((BLOCK_ROWS, width), lambda i: (i, 0)),
             pl.BlockSpec((entries, width), lambda i: (0, 0)),
         ]
-        + [pl.BlockSpec((span, width), lambda i: (0, 0))] * count,
+        + [pl.BlockSpec((span, width), lambda i: (0, 0))] * given,
         out_specs=(
             pl.BlockSpec((BLOCK_ROWS, row_count), lambda i: (i, 0)),
             pl.BlockSpec((row_count, width), lambda i: (0, 0)),
@@ -364,7 +389,7 @@
             pltpu.VMEM((1, row_count), jnp.float32),
             pltpu.VMEM((1, row_count), jnp.float32),
         ],
-    )(weight, label_weight, *pieces)
+    )(member, weight, label_weight, *pieces)
 
 
 def log_add(first, second):
@@ -380,14 +405,14 @@
 
 
 def ctc_pass(stats, slots, labels, frame_counts, label_counts, frame_count, label_max):
-    sources = len(stats)
-    count, _, span = stats[0].shape
-    row_count = count * span
+    group_count, sources = len(stats), len(stats[0])
+    count, _, span = stats[0][0].shape
+    row_count = group_count * count * span
     utterances = labels.shape[0]
     entries = utterances * COLS
+    given = group_count * sources
 
     def kernel(slots_ref, labels_ref, frames_ref, counts_ref, *refs):
-        stats_refs = refs[:sources]
         (
             out_ref,
             high_ref,
@@ -395,99 +420,100 @@
             loss_ref,
             turn_ref,
             emission_ref,
+            emit_blank,
+            emit_label,
             blank_fwd,
             label_fwd,
             blank_bwd,
             label_bwd,
             occupancy_ref,
-        ) = refs[sources:]
+        ) = refs[given:]
         place = lax.broadcasted_iota(jnp.int32, (COLS, span), 0)
         turn_ref[...] = jnp.zeros(turn_ref.shape, jnp.float32)
-        for slot in range(count):
-            found = [stats_refs[k][slots_ref[k * count + slot]] for k in range(sources)]
+        for part in range(group_count * count):
+            group, slot = part // count, part % count
+            found = [
+                refs[group * sources + k][slots_ref[k * count + slot]] for k in range(sources)
+            ]
             joined = found[0]
             peak = found[0][PEAK : PEAK + 1]
-            for part in found[1:]:
-                joined = joined + part
-                peak = jnp.maximum(peak, part[PEAK : PEAK + 1])
+            for other in found[1:]:
+                joined = joined + other
+                peak = jnp.maximum(peak, other[PEAK : PEAK + 1])
             total = jnp.zeros((1, span), jnp.float32)
-            for part in found:
-                total = total + part[TOTAL : TOTAL + 1] * jnp.exp(part[PEAK : PEAK + 1] - peak)
+            for other in found:
+                total = total + other[TOTAL : TOTAL + 1] * jnp.exp(other[PEAK : PEAK + 1] - peak)
             log_total = peak + jnp.log(total)
             turn_ref[:COLS, :span] = jnp.where(place == TOTAL, log_total, joined - log_total)
-            emission_ref[slot * span : (slot + 1) * span] = jnp.transpose(turn_ref[...], (1, 0))[
+            emission_ref[part * span : (part + 1) * span] = jnp.transpose(turn_ref[...], (1, 0))[
                 :span
             ]
 
-        lane = lax.broadcasted_iota(jnp.int32, (utterances, 128), 1)
+        lane = lax.broadcasted_iota(jnp.int32, (utterances, LANES), 1)
         is_label = lane < label_max
         is_blank = lane <= label_max
         names = labels_ref[...]
         earlier = pltpu.roll(names, 1, 1)
         skip = is_label & (lane >= 1) & (names != 0) & (names != earlier)
-        later = pltpu.roll(names, 127, 1)
+        later = pltpu.roll(names, LANES - 1, 1)
         skip_next = (lane < label_max - 1) & (later != 0) & (later != names)
         frames = frames_ref[...]
         counts = counts_ref[...]
-        lowest = jnp.full((utterances, 128), LOG_ZERO, jnp.float32)
         ends_blank = jnp.where(lane == counts, 0.0, LOG_ZERO)
         ends_label = jnp.where(lane == counts - 1, 0.0, LOG_ZERO)
 
-        def emitted(step):
+        def spread(step, carry):
             row = emission_ref[pl.ds(step, utterances, stride=frame_count), :]
             blank = jnp.sum(jnp.where(lane == label_max, row, 0.0), axis=1, keepdims=True)
-            return (
-                jnp.where(is_blank, blank, LOG_ZERO),
-                jnp.where(is_label, row, LOG_ZERO),
-            )
+            emit_blank[step] = jnp.where(is_blank, blank, LOG_ZERO)
+            emit_label[step] = jnp.where(is_label, row, LOG_ZERO)
+            return carry
+
+        lax.fori_loop(0, frame_count, spread, 0, unroll=16)
 
         def advance(step, carry):
             fwd_blank, fwd_label, bwd_blank, bwd_label = carry
-            emit_blank, emit_label = emitted(step)
             moved = jnp.where(lane == 0, LOG_ZERO, pltpu.roll(fwd_label, 1, 1))
-            new_blank = log_add(fwd_blank, moved) + emit_blank
+            new_blank = log_add(fwd_blank, moved) + emit_blank[step]
             new_label = (
-                log_add3(fwd_label, fwd_blank, jnp.where(skip, moved, LOG_ZERO)) + emit_label
+                log_add3(fwd_label, fwd_blank, jnp.where(skip, moved, LOG_ZERO))
+                + emit_label[step]
             )
-            start_blank = jnp.where(lane == 0, emit_blank, LOG_ZERO)
-            start_label = jnp.where(lane == 0, emit_label, LOG_ZERO)
-            first = step == 0
-            new_blank = jnp.where(first, start_blank, new_blank)
-            new_label = jnp.where(first, start_label, new_label)
             alive = step < frames
-            fwd_blank = jnp.where(alive, jnp.where(is_blank, new_blank, LOG_ZERO), fwd_blank)
-            fwd_label = jnp.where(alive, jnp.where(is_label, new_label, LOG_ZERO), fwd_label)
+            fwd_blank = jnp.where(alive, new_blank, fwd_blank)
+            fwd_label = jnp.where(alive, new_label, fwd_label)
             blank_fwd[step] = fwd_blank
             label_fwd[step] = fwd_label
 
             back = frame_count - 1 - step
-            emit_blank, emit_label = emitted(jnp.minimum(back + 1, frame_count - 1))
-            out_blank = bwd_blank + emit_blank
-            out_label = bwd_label + emit_label
-            next_blank = pltpu.roll(out_blank, 127, 1)
-            next_label = jnp.where(skip_next, pltpu.roll(out_label, 127, 1), LOG_ZERO)
-            new_blank = log_add(out_blank, out_label)
-            new_label = log_add3(out_label, next_blank, next_label)
-            last = back == frames - 1
-            inside = back < frames - 1
-            bwd_blank = jnp.where(last, ends_blank, jnp.where(inside, new_blank, LOG_ZERO))
-            bwd_label = jnp.where(last, ends_label, jnp.where(inside, new_label, LOG_ZERO))
-            bwd_blank = jnp.where(is_blank, bwd_blank, LOG_ZERO)
-            bwd_label = jnp.where(is_label, bwd_label, LOG_ZERO)
+            out_blank = bwd_blank + emit_blank[back + 1]
+            out_label = bwd_label + emit_label[back + 1]
+            next_blank = pltpu.roll(out_blank, LANES - 1, 1)
+            next_label = jnp.where(skip_next, pltpu.roll(out_label, LANES - 1, 1), LOG_ZERO)
+            ended = back >= frames - 1
+            bwd_blank = jnp.where(ended, ends_blank, log_add(out_blank, out_label))
+            bwd_label = jnp.where(
+                ended, ends_label, log_add3(out_label, next_blank, next_label)
+            )
             blank_bwd[back] = bwd_blank
             label_bwd[back] = bwd_label
             return (fwd_blank, fwd_label, bwd_blank, bwd_label)
 
+        first_blank = jnp.where(lane == 0, emit_blank[0], LOG_ZERO)
+        first_label = jnp.where(lane == 0, emit_label[0], LOG_ZERO)
+        blank_fwd[0] = first_blank
+        label_fwd[0] = first_label
+        blank_bwd[frame_count - 1] = ends_blank
+        label_bwd[frame_count - 1] = ends_label
         fwd_blank, fwd_label, _, _ = lax.fori_loop(
-            0, frame_count, advance, (lowest, lowest, lowest, lowest)
+            1, frame_count, advance, (first_blank, first_label, ends_blank, ends_label), unroll=4
         )
         end_state = jnp.sum(jnp.where(lane == counts, fwd_blank, 0.0), axis=1, keepdims=True)
         near_state = jnp.sum(jnp.where(lane == counts - 1, fwd_label, 0.0), axis=1, keepdims=True)
         log_like = log_add(end_state, near_state)
-        loss_ref[...] = jnp.broadcast_to(-log_like, (utterances, 128))
+        loss_ref[...] = jnp.broadcast_to(-log_like, (utterances, LANES))
 
         def occupy(step, carry):
-            alive = step < frames
             blank = jnp.exp(blank_fwd[step] + blank_bwd[step] - log_like)
             label = jnp.exp(label_fwd[step] + label_bwd[step] - log_like)
             blank = jnp.sum(jnp.where(is_blank, blank, 0.0), axis=1, keepdims=True)
@@ -495,14 +521,14 @@
             whole = blank + jnp.sum(label, axis=1, keepdims=True)
             filled = jnp.where(lane == label_max, blank, label)
             filled = jnp.where(lane == WHOLE, whole, filled)
-            filled = jnp.where(alive, -filled, 0.0)
+            filled = jnp.where(step < frames, -filled, 0.0)
             row = emission_ref[pl.ds(step, utterances, stride=frame_count), :]
             occupancy_ref[pl.ds(step, utterances, stride=frame_count), :] = jnp.where(
                 lane == TOTAL, row, filled
             )
             return carry
 
-        lax.fori_loop(0, frame_count, occupy, 0, unroll=8)
+        lax.fori_loop(0, frame_count, occupy, 0, unroll=16)
         turned = jnp.transpose(occupancy_ref[...], (1, 0))[:COLS]
         out_ref[...] = turned
         row_place = lax.broadcasted_iota(jnp.int32, (COLS, row_count), 0)
@@ -516,90 +542,82 @@
                 part - high.astype(jnp.float32)
             ).astype(jnp.bfloat16)
 
-    held = pltpu.VMEM((frame_count, utterances, 128), jnp.float32)
+    held = pltpu.VMEM((frame_count, utterances, LANES), jnp.float32)
+    table = pltpu.VMEM((row_count, LANES), jnp.float32)
+    flat = [value for group in stats for value in group]
     return call(
         kernel,
         (
             jax.ShapeDtypeStruct((COLS, row_count), jnp.float32),
             bf16_rows(entries, row_count),
             bf16_rows(entries, row_count),
-            jax.ShapeDtypeStruct((utterances, 128), jnp.float32),
+            jax.ShapeDtypeStruct((utterances, LANES), jnp.float32),
         ),
         1 << 26,
         1 << 20,
-        in_specs=[smem_spec()] + [vmem_spec()] * (3 + sources),
+        in_specs=[smem_spec()] + [vmem_spec()] * (3 + given),
         out_specs=tuple(vmem_spec() for _ in range(4)),
-        scratch_shapes=[
-            pltpu.VMEM((128, 128), jnp.float32),
-            pltpu.VMEM((row_count, 128), jnp.float32),
-            held,
-            held,
-            held,
-            held,
-            pltpu.VMEM((row_count, 128), jnp.float32),
-        ],
-    )(slots, labels, frame_counts, label_counts, *stats)
-
-
-def head_gradient(groups, order, blocks):
-    count = len(groups)
-    row_count, width = groups[0]["rows"].shape
-    entries = groups[0]["places"].shape[1]
-    names = ("logits", "rows", "out", "high", "low", "places")
+        scratch_shapes=[pltpu.VMEM((LANES, LANES), jnp.float32), table]
+        + [held] * 6
+        + [table],
+    )(slots, labels, frame_counts, label_counts, *flat)
+
+
+def head_gradient(logits, rows, occupancy, high, low, places, order, blocks):
+    count = len(logits)
+    row_count, width = rows[0].shape
+    whole_count = count * row_count
+    entries = places.shape[1]
 
     def kernel(order_ref, *refs):
-        out_ref, rows_ref = refs[count * len(names) :]
-        sets = [
-            dict(zip(names, refs[g * len(names) : (g + 1) * len(names)])) for g in range(count)
-        ]
+        logits_refs, rows_refs = refs[:count], refs[count : 2 * count]
+        occupancy_ref, high_ref, low_ref, places_ref, out_ref, joined_ref = refs[2 * count :]
         step = pl.program_id(0)
 
         @pl.when(step == 0)
         def _():
-            for g, held in enumerate(sets):
-                rows_ref[g * row_count : (g + 1) * row_count] = held["rows"][...]
+            for g in range(count):
+                joined_ref[g * row_count : (g + 1) * row_count] = rows_refs[g][...]
 
         entry = order_ref[step] * BLOCK_ROWS + lax.broadcasted_iota(
             jnp.int32, (BLOCK_ROWS, entries), 0
         )
-        grads = []
-        for held in sets:
-            select = as_mask(entry == held["places"][...])
-            scattered = lax.dot_general(
-                select, held["high"][...], NN, preferred_element_type=jnp.float32
-            ) + lax.dot_general(select, held["low"][...], NN, preferred_element_type=jnp.float32)
-            whole = held["out"][WHOLE : WHOLE + 1]
-            log_total = held["out"][TOTAL : TOTAL + 1]
-            grad = scattered - jnp.exp(held["logits"][...] - log_total) * whole
-            grads.append(grad.astype(jnp.bfloat16))
+        select = as_mask(entry == places_ref[...])
+        scattered = lax.dot_general(
+            select, high_ref[...], NN, preferred_element_type=jnp.float32
+        ) + lax.dot_general(select, low_ref[...], NN, preferred_element_type=jnp.float32)
+        values = jnp.concatenate([ref[...] for ref in logits_refs], axis=1)
+        whole = occupancy_ref[WHOLE : WHOLE + 1]
+        log_total = occupancy_ref[TOTAL : TOTAL + 1]
+        grad = (scattered - jnp.exp(values - log_total) * whole).astype(jnp.bfloat16)
         out_ref[...] = lax.dot_general(
-            jnp.concatenate(grads, axis=1),
-            rows_ref[...],
-            NN,
-            preferred_element_type=jnp.float32,
+            grad, joined_ref[...], NN, preferred_element_type=jnp.float32
         ).astype(jnp.bfloat16)
 
-    specs = [
-        pl.BlockSpec((BLOCK_ROWS, row_count), lambda i, order: (order[i], 0)),
-        pl.BlockSpec((row_count, width), lambda i, order: (0, 0)),
-        pl.BlockSpec((COLS, row_count), lambda i, order: (0, 0)),
-        pl.BlockSpec((entries, row_count), lambda i, order: (0, 0)),
-        pl.BlockSpec((entries, row_count), lambda i, order: (0, 0)),
-        pl.BlockSpec((1, entries), lambda i, order: (0, 0)),
-    ]
+    def fixed(*shape):
+        return pl.BlockSpec(shape, lambda i, order: (0, 0))
+
     return call(
         kernel,
         bf16_rows(blocks * BLOCK_ROWS, width),
-        2 * blocks * BLOCK_ROWS * row_count * count * (width + 2 * entries),
+        2 * blocks * BLOCK_ROWS * whole_count * (width + 2 * entries),
         10 << 20,
+        STREAM_LIMIT,
         grid_spec=pltpu.PrefetchScalarGridSpec(
             num_scalar_prefetch=1,
             grid=(blocks,),
-            in_specs=specs * count,
+            in_specs=[pl.BlockSpec((BLOCK_ROWS, row_count), lambda i, order: (order[i], 0))] * count
+            + [fixed(row_count, width)] * count
+            + [
+                fixed(COLS, whole_count),
+                fixed(entries, whole_count),
+                fixed(entries, whole_count),
+                fixed(1, entries),
+            ],
             out_specs=pl.BlockSpec((BLOCK_ROWS, width), lambda i, order: (i, 0)),
-            scratch_shapes=[pltpu.VMEM((count * row_count, width), jnp.bfloat16)],
+            scratch_shapes=[pltpu.VMEM((whole_count, width), jnp.bfloat16)],
         ),
-    )(order, *[group[name] for group in groups for name in names])
+    )(order, *logits, *rows, occupancy, high, low, places)
 
 
 def assemble(pieces, offsets, height):
@@ -657,18 +675,24 @@
     return lax.ppermute(value, axis, [(i, (i + by) % count) for i in range(count)])
 
 
-def spread_rows(value, member):
+def after(value, *others):
+    return lax.optimization_barrier((value,) + others)[0]
+
+
+def line_near(value):
     left = lax.ppermute(value, "expert", [(1, 0), (2, 1), (3, 2)])
     right = lax.ppermute(value, "expert", [(0, 1), (1, 2), (2, 3)])
-    left_far = lax.ppermute(left, "expert", [(1, 0), (2, 1)])
-    right_far = lax.ppermute(right, "expert", [(1, 2), (2, 3)])
-    low = member < 2
-    near = jnp.where(low, left, right)
-    far = jnp.where(low, left_far, right_far)
-    end = lax.ppermute(far, "expert", [(1, 0), (2, 3)])
-    passed = jnp.where(low, right, left)
-    last = jnp.where((member == 0) | (member == 3), end, passed)
-    return [value, near, far, last]
+    return left, right
+
+
+def line_far(near, member):
+    left = lax.ppermute(near[0], "expert", [(1, 0), (2, 1)])
+    right = lax.ppermute(near[1], "expert", [(1, 2), (2, 3)])
+    return jnp.where(member < 2, left, right)
+
+
+def line_end(far):
+    return lax.ppermute(far, "expert", [(1, 0), (2, 3)])
 
 
 LINE_ORDER = np.array([[0, 1, 2, 3], [1, 2, 3, 0], [2, 1, 0, 3], [3, 2, 1, 0]])
@@ -730,55 +754,14 @@
     def mine_of(value):
         return lax.dynamic_slice_in_dim(value, first_pair, per_section, 0)
 
-    own_ids = routing.reshape(pair_count, frame_count)
-    own_table = jnp.concatenate(
-        [
-            norm_gain,
-            jnp.zeros((7, width), jnp.float32),
-            jnp.transpose(router[0]).astype(jnp.float32),
-            jnp.zeros((round_up(experts, 8) - experts, width), jnp.float32),
-        ],
-        axis=0,
-    )
-    own = (w_in[0, 0], w_out[0, 0])
-    paired = sections == 2 and inner_size == 2
-    if paired:
-        other_ids = swap(own_ids, "section")
-        other_table = swap(own_table, "section")
-        half = hidden // 2
-        sent_in = lax.dynamic_slice(own[0], (0, core * half), (width, half))
-        sent_out = lax.dynamic_slice(own[1], (core * half, 0), (half, width))
-        sent_in, sent_out, other_ids, other_table = lax.optimization_barrier(
-            (sent_in, sent_out, other_ids, other_table)
-        )
-        came_in = swap(sent_in, "section")
-        came_out = swap(sent_out, "section")
-        other = [(came_in, came_out), (swap(came_in, "dpi"), swap(came_out, "dpi"))]
-    else:
-        all_ids = lax.all_gather(own_ids, "section")
-        all_tables = lax.all_gather(own_table, "section")
-        all_in = lax.all_gather(own[0], "section")
-        all_out = lax.all_gather(own[1], "section")
-
-    def of_layer(layer):
-        if not paired:
-            chosen = (all_in[layer], all_out[layer])
-            return all_ids[layer], all_tables[layer], chosen, [], jnp.ones((1,), jnp.int32)
-        mine = section_id == layer
-        return (
-            jnp.where(mine, own_ids, other_ids),
-            jnp.where(mine, own_table, other_table),
-            own,
-            other,
-            mine.astype(jnp.int32).reshape(1),
-        )
-
-    layers = []
-    for layer in range(sections):
-        ids, table, weights, others, pick_own = of_layer(layer)
+    def exchange(blocks, sign):
+        return [blocks[0]] + [
+            rotate(blocks[k], "expert", sign * k) for k in range(1, group_size)
+        ]
+
+    def lanes_of(ids):
         ids = jnp.pad(mine_of(ids), ((0, 0), (0, LANES - frame_count)), constant_values=-1)
-        parts = [ids[g * group_pairs : (g + 1) * group_pairs] for g in range(group_count)]
-        layers.append((parts, table, weights, others, pick_own))
+        return [ids[g * group_pairs : (g + 1) * group_pairs] for g in range(group_count)]
 
     rows = lax.dynamic_slice_in_dim(
         frames.reshape(pair_count * frame_count, width),
@@ -787,18 +770,62 @@
         0,
     )
     current = [rows[g * span : (g + 1) * span] for g in range(group_count)]
-
-    def exchange(blocks, sign):
-        return [blocks[0]] + [
-            rotate(blocks[k], "expert", sign * k) for k in range(1, group_size)
+    own_ids = routing.reshape(pair_count, frame_count)
+    paired = sections == 2 and inner_size == 2
+    if paired:
+        other_ids = swap(own_ids, "section")
+        all_ids = [
+            jnp.where(section_id == layer, own_ids, other_ids) for layer in range(sections)
         ]
-
+    else:
+        all_ids = lax.all_gather(own_ids, "section")
+    layer_ids = [lanes_of(all_ids[layer]) for layer in range(sections)]
     outgoing = [
-        dispatch(current[g], layers[0][0][g], member_ref, experts, capacity, frame_count)
+        dispatch(current[g], layer_ids[0][g], member_ref, experts, capacity, frame_count)
         for g in range(group_count)
     ]
     received = [exchange(blocks, 1) for blocks in outgoing]
 
+    held_gain, held_router, held_in, held_out = lax.optimization_barrier(
+        (norm_gain, router, w_in, w_out, outgoing[0][0])
+    )[:4]
+    own_table = jnp.concatenate(
+        [
+            held_gain,
+            jnp.zeros((7, width), jnp.float32),
+            jnp.transpose(held_router[0]).astype(jnp.float32),
+            jnp.zeros((round_up(experts, 8) - experts, width), jnp.float32),
+        ],
+        axis=0,
+    )
+    own = (held_in[0, 0], held_out[0, 0])
+    if paired:
+        other_table = swap(own_table, "section")
+        half = hidden // 2
+        sent_in = lax.dynamic_slice(own[0], (0, core * half), (width, half))
+        sent_out = lax.dynamic_slice(own[1], (core * half, 0), (half, width))
+        sent_in, sent_out, other_table = lax.optimization_barrier((sent_in, sent_out, other_table))
+        came_in = swap(sent_in, "section")
+        came_out = swap(sent_out, "section")
+        other = [(came_in, came_out), (swap(came_in, "dpi"), swap(came_out, "dpi"))]
+    else:
+        all_tables = lax.all_gather(own_table, "section")
+        all_in = lax.all_gather(own[0], "section")
+        all_out = lax.all_gather(own[1], "section")
+
+    layers = []
+    for layer in range(sections):
+        if paired:
+            mine = section_id == layer
+            table = jnp.where(mine, own_table, other_table)
+            layers.append((table, own, other, mine.astype(jnp.int32).reshape(1)))
+        else:
+            chosen = (all_in[layer], all_out[layer])
+            layers.append((all_tables[layer], chosen, [], jnp.ones((1,), jnp.int32)))
+
+    labels, frame_lengths, label_lengths = lax.optimization_barrier(
+        (labels, frame_lengths, label_lengths, outgoing[-1][0])
+    )[:3]
     notes = jnp.concatenate(
         [
             mine_of(labels.reshape(pair_count, label_max)),
@@ -822,49 +849,39 @@
         notes_all = lax.all_gather(notes, "expert")
     shard = head_weight.shape[1]
     weight_rows = jnp.transpose(head_weight)
-    known, all_places = [], []
-    for g in range(group_count):
-        part = notes_all[:, g * group_pairs : (g + 1) * group_pairs].reshape(
-            group_size * group_pairs, label_max + 2
-        )
-        utterances = part.shape[0]
-        names = part[:, :label_max]
-        named = jnp.concatenate(
-            [
-                names,
-                jnp.zeros((utterances, 1), jnp.int32),
-                jnp.full((utterances, COLS - label_max - 1), -1, jnp.int32),
-            ],
-            axis=1,
-        ).reshape(utterances * COLS)
-        local = named - member * shard
-        places = jnp.where((named >= 0) & (local >= 0) & (local < shard), local, -1)
-        all_places.append(places)
-        known.append(
-            (
-                jnp.pad(names, ((0, 0), (0, LANES - label_max))),
-                part[:, label_max : label_max + 1],
-                part[:, label_max + 1 :],
-                places.reshape(1, -1),
-            )
-        )
-    label_weight = label_rows(weight_rows, jnp.concatenate(all_places).reshape(-1, 1))
-    entries = all_places[0].shape[0]
-    received, label_weight = lax.optimization_barrier((received, label_weight))
-
-    spread = []
+    split = notes_all.reshape(group_size, group_count, group_pairs, label_max + 2)
+    notes_all = jnp.transpose(split, (1, 0, 2, 3)).reshape(-1, label_max + 2)
+    utterances = notes_all.shape[0]
+    names = notes_all[:, :label_max]
+    named = jnp.concatenate(
+        [
+            names,
+            jnp.zeros((utterances, 1), jnp.int32),
+            jnp.full((utterances, COLS - label_max - 1), -1, jnp.int32),
+        ],
+        axis=1,
+    ).reshape(utterances * COLS)
+    local = named - member * shard
+    places = jnp.where((named >= 0) & (local >= 0) & (local < shard), local, -1)
+    label_weight = label_rows(weight_rows, places.reshape(-1, 1))
+    entries = utterances * COLS // group_count
+
+    normed = []
     for layer in range(sections):
-        ids, table, weights, others, pick_own = layers[layer]
+        table, weights, others, pick_own = layers[layer]
+        ids = layer_ids[layer]
         for g in range(group_count):
             done = run_expert(received[g], table, weights, others, pick_own)
             returned = exchange(done, -1)
+            if layer == 0 and g == 0:
+                returned, label_weight = lax.optimization_barrier((returned, label_weight))
             if layer < sections - 1:
                 current[g], blocks = combine_and_dispatch(
                     current[g],
                     returned,
                     ids[g],
                     table,
-                    layers[layer + 1][0][g],
+                    layer_ids[layer + 1][g],
                     member_ref,
                     experts,
                     capacity,
@@ -872,65 +889,111 @@
                 )
                 received[g] = exchange(blocks, 1)
             else:
-                normed = combine_and_norm(
-                    current[g],
-                    returned,
-                    ids[g],
-                    table,
-                    head_gain.reshape(1, width),
-                    member_ref,
-                    experts,
-                    capacity,
-                    frame_count,
+                normed.append(
+                    combine_and_norm(
+                        current[g],
+                        returned,
+                        ids[g],
+                        table,
+                        head_gain.reshape(1, width),
+                        member_ref,
+                        experts,
+                        capacity,
+                        frame_count,
+                    )
                 )
-                if group_size == 4:
-                    spread.append(spread_rows(normed, member))
-                else:
-                    gathered = lax.all_gather(normed, "expert")
-                    spread.append([gathered[k] for k in range(group_size)])
-
+
+    def logits_of(g, pieces):
+        return head_logits(
+            pieces,
+            member_ref,
+            weight_rows,
+            label_weight[g * entries : (g + 1) * entries],
+            frame_count,
+        )
+
+    def stats_of(stats):
+        if group_size == 4:
+            return [stats] + [rotate(stats, "expert", -k) for k in range(1, group_size)]
+        gathered = lax.all_gather(stats, "expert")
+        return [
+            lax.dynamic_index_in_dim(gathered, (member + k) % group_size, 0, keepdims=False)
+            for k in range(group_size)
+        ]
+
+    heads, found = [], []
+    previous = None
+    for g in range(group_count):
+        value = normed[g]
+        if group_size == 4:
+            if previous is not None:
+                value = after(value, *previous[0])
+            near = line_near(value)
+            if previous is not None:
+                near = lax.optimization_barrier((near, previous[1]))[0]
+            far = line_far(near, member)
+            if previous is not None:
+                far = after(far, previous[2])
+            pieces = [value, *near, far, line_end(far)]
+        else:
+            gathered = lax.all_gather(value, "expert")
+            near, far = None, None
+            pieces = [gathered[k] for k in range(group_size)]
+        logits, rows_all, stats = logits_of(g, pieces)
+        previous = (near, far, stats)
+        heads.append((logits, rows_all))
+        found.append(stats_of(stats))
     tables = jnp.asarray(slot_tables(group_size))
     slots = lax.dynamic_index_in_dim(tables, member, 0, keepdims=False)
-    groups, my_losses = [], []
-    for g in range(group_count):
-        logits, rows_all, stats = head_logits(
-            spread[g], weight_rows, label_weight[g * entries : (g + 1) * entries], frame_count
-        )
-        if group_size == 4:
-            found = [stats] + [rotate(stats, "expert", -k) for k in range(1, group_size)]
-        else:
-            gathered = lax.all_gather(stats, "expert")
-            found = [
-                lax.dynamic_index_in_dim(gathered, (member + k) % group_size, 0, keepdims=False)
-                for k in range(group_size)
-            ]
-        names, frames_all, counts_all, places = known[g]
-        out, high, low, losses = ctc_pass(
-            found, slots, names, frames_all, counts_all, frame_count, label_max
-        )
-        own_slot = 0 if group_size == 4 else member
-        my_losses.append(
-            lax.dynamic_slice(losses, (own_slot * group_pairs, 0), (group_pairs, 1))
-        )
-        groups.append(
-            dict(logits=logits, rows=rows_all, out=out, high=high, low=low, places=places)
-        )
-    my_losses = jnp.concatenate(my_losses, axis=0)
-    blocks = groups[0]["logits"].shape[0] // BLOCK_ROWS
+    occupancy, high, low, losses = ctc_pass(
+        found,
+        slots,
+        jnp.pad(names, ((0, 0), (0, LANES - label_max))),
+        notes_all[:, label_max : label_max + 1],
+        notes_all[:, label_max + 1 :],
+        frame_count,
+        label_max,
+    )
+    own_slot = 0 if group_size == 4 else member
+    held_utterances = group_size * group_pairs
+    my_losses = jnp.concatenate(
+        [
+            lax.dynamic_slice(
+                losses, (g * held_utterances + own_slot * group_pairs, 0), (group_pairs, 1)
+            )
+            for g in range(group_count)
+        ],
+        axis=0,
+    )
+
+    def gradient(order, count):
+        return head_gradient(
+            [head[0] for head in heads],
+            [head[1] for head in heads],
+            occupancy,
+            high,
+            low,
+            places.reshape(1, -1),
+            order,
+            count,
+        )
+
+    blocks = heads[0][0].shape[0] // BLOCK_ROWS
     if paired and outer_size == 2 and blocks == 8:
         outer = lax.axis_index("dpo")
 
         def pair_of(side, first, second):
             return jnp.stack([side * 4 + first, side * 4 + 2 + second]).astype(jnp.int32)
 
-        sibling_sent = head_gradient(groups, pair_of(1 - core, 1 - section_id, 1 - outer), 2)
-        sibling_kept = head_gradient(groups, pair_of(1 - core, section_id, outer), 2)
+        sibling_sent = gradient(pair_of(1 - core, 1 - section_id, 1 - outer), 2)
         came_sent = swap(sibling_sent, "dpi")
-        came_kept = swap(sibling_kept, "dpi")
-        sent = add(head_gradient(groups, pair_of(core, 1 - section_id, 1 - outer), 2), came_sent)
+        own_order = after(pair_of(core, 1 - section_id, 1 - outer), sibling_sent)
+        sent = add(gradient(own_order, 2), came_sent)
         first_in = swap(sent[:BLOCK_ROWS], "section")
         second_in = swap(sent[BLOCK_ROWS:], "dpo")
-        kept = add(head_gradient(groups, pair_of(core, section_id, outer), 2), came_kept)
+        kept_order = after(pair_of(1 - core, section_id, outer), sent)
+        came_kept = swap(gradient(kept_order, 2), "dpi")
+        kept = add(gradient(after(pair_of(core, section_id, outer), sent), 2), came_kept)
         first = add(kept[:BLOCK_ROWS], first_in)
         second = add(kept[BLOCK_ROWS:], second_in)
         part = BLOCK_ROWS // 2
@@ -971,7 +1034,7 @@
             ]
         whole = assemble(pieces, jnp.stack(offsets).astype(jnp.int32), shard)
     else:
-        partial = head_gradient(groups, jnp.arange(blocks, dtype=jnp.int32), blocks)[:shard]
+        partial = gradient(jnp.arange(blocks, dtype=jnp.int32), blocks)[:shard]
         whole = lax.psum(partial.astype(jnp.float32), ("section", "dpo", "dpi")).astype(
             jnp.bfloat16
         )

time: 241 us -> 280 us (1.16)
  waiting for transfers between devices: 67 us -> 104 us
  Pallas kernels: 60.1 us -> 72.4 us
  local copies, waits for them, and re-layouts: 19.8 us -> 11.8 us
  starting transfers between devices: 85.2 us -> 78.2 us
  other arithmetic: 5.89 us -> 10.3 us
    ppermute x33, waiting for transfers between devices: 12.2 us -> 35 us  [rotate(): lax.ppermute(value, axis, [(i, (i + by) % count) for i in range(count)])]
    pallas_call x2 -> x1, Pallas kernels: 21.6 us -> 6.61 us  [ctc_pass(): call(kernel, (jax.ShapeDtypeStruct((COLS, row_count), jnp.float32), bf16_...]
    pallas_call x4, Pallas kernels: 12.2 us -> 23.3 us  [head_gradient(): call(kernel, bf16_rows(blocks * BLOCK_ROWS, width), 2 * blocks * BLOCK_RO...]
    pallas_call x2, Pallas kernels: 11.4 us -> 20.8 us  [head_logits(): call(kernel, (jax.ShapeDtypeStruct((blocks * BLOCK_ROWS, row_count), jnp....]
    ppermute x21, waiting for transfers between devices: 43 us -> 50.4 us  [swap(): return lax.ppermute(value, axis, [(0, 1), (1, 0)])]
    ppermute x10, waiting for transfers between devices: 11.8 us -> 18.8 us  [the longest x2 7.19 us: line_near(): left = lax.ppermute(value, 'expert', [(1, 0), (2, 1), (3, 2)])]
    unnamed x58 -> x74, local copies, waits for them, and re-layouts: 13 us -> 6.48 us
    ppermute x10, starting transfers between devices: 18.4 us -> 13.9 us  [the longest x2 4.15 us: line_near(): right = lax.ppermute(value, 'expert', [(0, 1), (1, 2), (2, 3)])]
  transfers between devices with their start and end apart: 64 -> 64, of which waited for: 18 -> 34; matrix products, arithmetic and copies ran while one was open for 5% -> 4% of each run, Pallas kernels for 18% -> 13%
where the time goes in v1:
time: 280 us; the launch traced here: 278 us
  waiting for transfers between devices  104 us (37%)
  starting transfers between devices  78.2 us (28%)
  Pallas kernels  72.4 us (26%)
  local copies, waits for them, and re-layouts  11.8 us (4%)
  other arithmetic  10.3 us (4%)
    ppermute x33, starting transfers between devices, rotate(): lax.ppermute(value, axis, [(i, (i + by) % count) for i in range(count)])  50.6 us
    ppermute x21, waiting for transfers between devices, swap(): return lax.ppermute(value, axis, [(0, 1), (1, 0)])  50.4 us
    ppermute x33, waiting for transfers between devices, rotate(): lax.ppermute(value, axis, [(i, (i + by) % count) for i in range(count)])  35 us
    pallas_call x4, Pallas kernels, head_gradient(): call(kernel, bf16_rows(blocks * BLOCK_ROWS, width), 2 * blocks * BLOCK_RO...  23.3 us
    pallas_call x2, Pallas kernels, head_logits(): call(kernel, (jax.ShapeDtypeStruct((blocks * BLOCK_ROWS, row_count), jnp....  20.8 us
    ppermute x21, starting transfers between devices, swap(): return lax.ppermute(value, axis, [(0, 1), (1, 0)])  13.7 us
    pallas_call x1, Pallas kernels, label_rows(): call(kernel, bf16_rows(entries, width), 2 * blocks * BLOCK_ROWS * entries...  7.89 us
    ppermute x2, waiting for transfers between devices, line_near(): left = lax.ppermute(value, 'expert', [(1, 0), (2, 1), (3, 2)])  7.19 us
  transfers between devices with their start and end apart: 64, of which 34 were waited for; matrix products, arithmetic and copies ran while one was open for 4% of the time, Pallas kernels for 13%

profile of v1, /device:TPU:0, one launch (start us, length us, event | category | flops | bytes accessed | tf_op | source)
XLA Modules:
  0.0 278.3 jit_solution(8689447468218011916)
XLA Ops:
  0.7 3.0 %collective-permute-start = (s32[8,48]{1,0:T(8,128)}, s32[8,48]{1,0:T(8,128)S(1)}, u32[]{:S(2)}, u32[]{:S(2)}) collective-permute-start(s32[8,48]{1,0:T(8,128)} %bitcast.75), channel_id=1, source_target_pairs={{0,16},{16,0},{1,17},{17,1},{2,18},{18,2},{3,19},{19,3},{4,20},{20... | collective-permute-start | bytes 4616 | tf_op jit(solution)/shard_map/ppermute | solution.py:670
  8.0 3.1 %collective-permute-start.3 = (s32[4,14]{1,0:T(4,128)S(1)}, s32[4,14]{1,0:T(4,128)S(1)}, u32[]{:S(2)}, u32[]{:S(2)}) collective-permute-start(s32[4,14]{1,0:T(4,128)S(1)} %pad_add_fusion), channel_id=1, source_target_pairs={{0,8},{4,12},{8,0},{12,4},{1,9},{5,13},{9,1},{13,5},{2,10},{6,14},... | collective-permute-start | bytes 680 | tf_op jit(solution)/shard_map/ppermute | solution.py:675
  19.5 3.3 %collective-permute-start.11 = (bf16[32,1280]{1,0:T(8,128)(2,1)}, bf16[32,1280]{1,0:T(8,128)(2,1)}, u32[]{:S(2)}, u32[]{:S(2)}) collective-permute-start(bf16[32,1280]{1,0:T(8,128)(2,1)} %get-tuple-element.82), channel_id=1, source_target_pairs={{0,12},{4,0},{8,4},{12,8},{1,13},{5,1},{9,5},{13,9},{2,14},{6,2},{... | collective-permute-start | bytes 245768 | tf_op jit(solution)/shard_map/ppermute | solution.py:675
  25.9 7.4 %collective-permute-done.5.refs_0_ = bf16[1280,128]{1,0:T(8,128)(2,1)S(1)} collective-permute-done((bf16[1280,128]{1,0:T(8,128)(2,1)}, bf16[1280,128]{1,0:T(8,128)(2,1)S(1)}, u32[]{:S(2)}, u32[]{:S(2)}) %collective-permute-start.5) | collective-permute-done | bytes 327712 | tf_op jit(solution)/shard_map/ppermute | solution.py:670
  33.3 3.5 %collective-permute-done.6.refs_1_ = bf16[128,1280]{1,0:T(8,128)(2,1)S(1)} collective-permute-done((bf16[128,1280]{1,0:T(8,128)(2,1)S(1)}, bf16[128,1280]{1,0:T(8,128)(2,1)S(1)}, u32[]{:S(2)}, u32[]{:S(2)}) %collective-permute-start.6) | collective-permute-done | bytes 327712 | tf_op jit(solution)/shard_map/ppermute | solution.py:670
  43.8 7.9 %shard_map.134 = bf16[256,1280]{1,0:T(8,128)(2,1)} custom-call(s32[256,1]{1,0:T(8,128)} %and_select_fusion.places_ref, bf16[2000,1280]{1,0:T(8,128)(2,1)} %bitcast.64), custom_call_target="tpu_custom_call" | custom-call | flops 1342177280 | bytes 6291456 | tf_op jit(solution)/shard_map/pallas_call | solution.py:275
  58.3 3.2 %collective-permute-done.15.refs_5_ = bf16[32,1280]{1,0:T(8,128)(2,1)S(1)} collective-permute-done((bf16[32,1280]{1,0:T(8,128)(2,1)}, bf16[32,1280]{1,0:T(8,128)(2,1)S(1)}, u32[]{:S(2)}, u32[]{:S(2)}) %collective-permute-start.15) | collective-permute-done | bytes 81952 | tf_op jit(solution)/shard_map/ppermute | solution.py:675
  64.1 3.0 %collective-permute-start.18 = (bf16[32,1280]{1,0:T(8,128)(2,1)S(1)}, bf16[32,1280]{1,0:T(8,128)(2,1)S(1)}, u32[]{:S(2)}, u32[]{:S(2)}) collective-permute-start(bf16[32,1280]{1,0:T(8,128)(2,1)S(1)} %get-tuple-element.98), channel_id=1, source_target_pairs={{0,12},{4,0},{8,4},{12,8},{1,13},{5,1},{9,5},{13,9},{2,14},{6,2},{... | collective-permute-start | bytes 245768 | tf_op jit(solution)/shard_map/ppermute | solution.py:675
  70.0 4.6 %collective-permute-done.19.refs_2_ = bf16[32,1280]{1,0:T(8,128)(2,1)S(1)} collective-permute-done((bf16[32,1280]{1,0:T(8,128)(2,1)S(1)}, bf16[32,1280]{1,0:T(8,128)(2,1)S(1)}, u32[]{:S(2)}, u32[]{:S(2)}) %collective-permute-start.19) | collective-permute-done | bytes 81952 | tf_op jit(solution)/shard_map/ppermute | solution.py:675
  86.1 5.2 %collective-permute-done.29.refs_5_ = bf16[32,1280]{1,0:T(8,128)(2,1)S(1)} collective-permute-done((bf16[32,1280]{1,0:T(8,128)(2,1)S(1)}, bf16[32,1280]{1,0:T(8,128)(2,1)S(1)}, u32[]{:S(2)}, u32[]{:S(2)}) %collective-permute-start.29) | collective-permute-done | bytes 81952 | tf_op jit(solution)/shard_map/ppermute | solution.py:675
  91.3 2.7 collective-permute-done.30.refs_6_
  95.0 2.8 collective-permute-start.33
  109.3 2.9 %collective-permute-start.37 = (bf16[32,1280]{1,0:T(8,128)(2,1)S(1)}, bf16[32,1280]{1,0:T(8,128)(2,1)S(1)}, u32[]{:S(2)}, u32[]{:S(2)}) collective-permute-start(bf16[32,1280]{1,0:T(8,128)(2,1)S(1)} %get-tuple-element.113), channel_id=1, source_target_pairs={{0,12},{4,0},{8,4},{12,8},{1,13},{5,1},{9,5},{13,9},{2,14},{6,2},{... | collective-permute-start | bytes 245768 | tf_op jit(solution)/shard_map/ppermute | solution.py:675
  112.8 3.2 %collective-permute-done.36.refs_6_ = bf16[32,1280]{1,0:T(8,128)(2,1)S(1)} collective-permute-done((bf16[32,1280]{1,0:T(8,128)(2,1)S(1)}, bf16[32,1280]{1,0:T(8,128)(2,1)S(1)}, u32[]{:S(2)}, u32[]{:S(2)}) %collective-permute-start.36) | collective-permute-done | bytes 81952 | tf_op jit(solution)/shard_map/ppermute | solution.py:675
  121.7 3.0 %collective-permute-done.39.refs_2_ = bf16[32,1280]{1,0:T(8,128)(2,1)S(1)} collective-permute-done((bf16[32,1280]{1,0:T(8,128)(2,1)S(1)}, bf16[32,1280]{1,0:T(8,128)(2,1)S(1)}, u32[]{:S(2)}, u32[]{:S(2)}) %collective-permute-start.39) | collective-permute-done | bytes 81952 | tf_op jit(solution)/shard_map/ppermute | solution.py:675
  131.9 7.2 %collective-permute-done.41.refs_1_ = bf16[96,1280]{1,0:T(8,128)(2,1)S(1)} collective-permute-done((bf16[96,1280]{1,0:T(8,128)(2,1)S(1)}, bf16[96,1280]{1,0:T(8,128)(2,1)S(1)}, u32[]{:S(2)}, u32[]{:S(2)}) %collective-permute-start.41) | collective-permute-done | bytes 245792 | tf_op jit(solution)/shard_map/ppermute | solution.py:683
  143.3 3.9 %collective-permute-done.43 = bf16[96,1280]{1,0:T(8,128)(2,1)S(1)} collective-permute-done((bf16[96,1280]{1,0:T(8,128)(2,1)S(1)}, bf16[96,1280]{1,0:T(8,128)(2,1)S(1)}, u32[]{:S(2)}, u32[]{:S(2)}) %collective-permute-start.43) | collective-permute-done | bytes 245792 | tf_op jit(solution)/shard_map/ppermute | solution.py:689
  147.3 5.8 %collective-permute-done.25.refs_4_ = bf16[96,1280]{1,0:T(8,128)(2,1)S(1)} collective-permute-done((bf16[96,1280]{1,0:T(8,128)(2,1)S(1)}, bf16[96,1280]{1,0:T(8,128)(2,1)S(1)}, u32[]{:S(2)}, u32[]{:S(2)}) %collective-permute-start.25) | collective-permute-done | bytes 245792 | tf_op jit(solution)/shard_map/ppermute | solution.py:695
  153.8 10.4 %shard_map.138 = (f32[2048,384]{1,0:T(8,128)}, bf16[384,1280]{1,0:T(8,128)(2,1)}, f32[4,16,96]{2,1,0:T(8,128)}) custom-call(s32[1]{0:T(128)} %bitcast.1.member_ref, bf16[2000,1280]{1,0:T(8,128)(2,1)} %bitcast.65, bf16[128,1280]{1,0:T(8,128)(2,1)} %get-tuple-element.155.label_ref, bf16[96,1280]{1,0:T(8,128)(2,1)} %copy-done.8, ...), custom_call_target="tpu_custom_call" | custom-call | flops 2013265920 | bytes 9437184 | tf_op jit(solution)/shard_map/pallas_call | solution.py:366
  169.1 2.8 collective-permute-start.26
  173.3 10.5 %shard_map.143 = (f32[2048,384]{1,0:T(8,128)}, bf16[384,1280]{1,0:T(8,128)(2,1)}, f32[4,16,96]{2,1,0:T(8,128)}) custom-call(s32[1]{0:T(128)} %bitcast.1.member_ref, bf16[2000,1280]{1,0:T(8,128)(2,1)} %bitcast.66, bf16[128,1280]{1,0:T(8,128)(2,1)} %get-tuple-element.154.label_ref, bf16[96,1280]{1,0:T(8,128)(2,1)} %copy-done.9, bf16[96,1280]{1,0:T(8,128)(2,1)} %copy-done.34, ...), custom_call_target="tpu_custom_call" | custom-call | flops 2013265920 | bytes 9437184 | tf_op jit(solution)/shard_map/pallas_call | solution.py:366
  191.1 6.6 %shard_map.144 = (f32[16,768]{1,0:T(8,128)S(1)}, bf16[256,768]{1,0:T(8,128)(2,1)S(1)}, bf16[256,768]{1,0:T(8,128)(2,1)S(1)}, f32[16,128]{1,0:T(8,128)S(1)}) custom-call(s32[16]{0:T(128)S(1)} %fusion.2.slots_ref, s32[16,128]{1,0:T(8,128)S(1)} %pad.12.labels_ref, s32[16,1]{1,0:T(8,128)S(1)} %get-tuple-element.163.frames_ref, ...), custom_call_target="tpu_custom_call" | custom-call | flops 67108864 | bytes 1048576 | tf_op jit(solution)/shard_map/pallas_call | solution.py:548
  199.9 5.8 %shard_map.145 = bf16[512,1280]{1,0:T(8,128)(2,1)} custom-call(s32[2]{0:T(128)} %pad_add_fusion.3.order_ref, f32[2048,384]{1,0:T(8,128)} %get-tuple-element.124.refs_0_, f32[2048,384]{1,0:T(8,128)} %get-tuple-element.125.refs_1_, bf16[384,1280]{1,0:T(8,128)(2,1)} %get-tuple-element.126.refs_2_, bf16[384,1280]{1,0:T(8,128)(2,1)} %get-tuple-element.127.refs_3_, ...), custom_call_target="tpu_custom_call" | custom-call | flops 1409286144 | bytes 10485760 | tf_op jit(solution)/shard_map/pallas_call | solution.py:600
  206.9 5.8 %shard_map.146 = bf16[512,1280]{1,0:T(8,128)(2,1)} custom-call(s32[2]{0:T(128)} %pad_add_fusion.2.order_ref, f32[2048,384]{1,0:T(8,128)} %get-tuple-element.124.refs_0_, f32[2048,384]{1,0:T(8,128)} %get-tuple-element.125.refs_1_, bf16[384,1280]{1,0:T(8,128)(2,1)} %get-tuple-element.126.refs_2_, bf16[384,1280]{1,0:T(8,128)(2,1)} %get-tuple-element.127.refs_3_, ...), custom_call_target="tpu_custom_call" | custom-call | flops 1409286144 | bytes 10485760 | tf_op jit(solution)/shard_map/pallas_call | solution.py:600
  214.3 5.8 %shard_map.148 = bf16[512,1280]{1,0:T(8,128)(2,1)} custom-call(s32[2]{0:T(128)} %get-tuple-element.133.order_ref, f32[2048,384]{1,0:T(8,128)} %get-tuple-element.124.refs_0_, f32[2048,384]{1,0:T(8,128)} %get-tuple-element.125.refs_1_, bf16[384,1280]{1,0:T(8,128)(2,1)} %get-tuple-element.126.refs_2_, bf16[384,1280]{1,0:T(8,128)(2,1)} %get-tuple-element.127.refs_3_, ...), custom_call_target="tpu_custom_call" | custom-call | flops 1409286144 | bytes 10485760 | tf_op jit(solution)/shard_map/pallas_call | solution.py:600
  223.0 5.8 %shard_map.147 = bf16[512,1280]{1,0:T(8,128)(2,1)} custom-call(s32[2]{0:T(128)} %get-tuple-element.132.order_ref, f32[2048,384]{1,0:T(8,128)} %get-tuple-element.124.refs_0_, f32[2048,384]{1,0:T(8,128)} %get-tuple-element.125.refs_1_, bf16[384,1280]{1,0:T(8,128)(2,1)} %get-tuple-element.126.refs_2_, bf16[384,1280]{1,0:T(8,128)(2,1)} %get-tuple-element.127.refs_3_, ...), custom_call_target="tpu_custom_call" | custom-call | flops 1409286144 | bytes 10485760 | tf_op jit(solution)/shard_map/pallas_call | solution.py:600
  230.4 7.1 %collective-permute-done.53 = bf16[256,1280]{1,0:T(8,128)(2,1)S(1)} collective-permute-done((bf16[256,1280]{1,0:T(8,128)(2,1)S(1)}, bf16[256,1280]{1,0:T(8,128)(2,1)S(1)}, u32[]{:S(2)}, u32[]{:S(2)}) %collective-permute-start.53) | collective-permute-done | bytes 655392 | tf_op jit(solution)/shard_map/ppermute | solution.py:670
  240.4 7.2 %collective-permute-done.52 = bf16[128,1280]{1,0:T(8,128)(2,1)S(1)} collective-permute-done((bf16[128,1280]{1,0:T(8,128)(2,1)S(1)}, bf16[128,1280]{1,0:T(8,128)(2,1)S(1)}, u32[]{:S(2)}, u32[]{:S(2)}) %collective-permute-start.52) | collective-permute-done | bytes 327712 | tf_op jit(solution)/shard_map/ppermute | solution.py:670
  251.2 11.4 %collective-permute-done.56 = bf16[256,1280]{1,0:T(8,128)(2,1)S(1)} collective-permute-done((bf16[256,1280]{1,0:T(8,128)(2,1)S(1)}, bf16[256,1280]{1,0:T(8,128)(2,1)S(1)}, u32[]{:S(2)}, u32[]{:S(2)}) %collective-permute-start.56) | collective-permute-done | bytes 655392 | tf_op jit(solution)/shard_map/ppermute | solution.py:670
  265.8 5.1 %collective-permute-done.57.refs_6_ = bf16[128,1280]{1,0:T(8,128)(2,1)S(1)} collective-permute-done((bf16[128,1280]{1,0:T(8,128)(2,1)S(1)}, bf16[128,1280]{1,0:T(8,128)(2,1)S(1)}, u32[]{:S(2)}, u32[]{:S(2)}) %collective-permute-start.57) | collective-permute-done | bytes 327712 | tf_op jit(solution)/shard_map/ppermute | solution.py:670
  270.9 2.7 collective-permute-done.58.refs_7_
  275.2 3.0 %shard_map.149 = bf16[2000,1280]{1,0:T(8,128)(2,1)} custom-call(s32[16]{0:T(128)S(1)} %stack.123.offsets_ref, bf16[128,1280]{1,0:T(8,128)(2,1)S(1)} %add_convert_fusion.5.refs_0_, bf16[128,1280]{1,0:T(8,128)(2,1)S(1)} %add_convert_fusion.4.refs_1_, bf16[128,1280]{1,0:T(8,128)(2,1)S(1)} %get-tuple-element.153.refs_2_, ...), custom_call_target="tpu_custom_call" | custom-call | bytes 10240000 | tf_op jit(solution)/shard_map/pallas_call | solution.py:658
  (254 shorter events, 111.1 us)
Async XLA Ops:
  8.0 14.8 %collective-permute-start.3 = (s32[4,14]{1,0:T(4,128)S(1)}, s32[4,14]{1,0:T(4,128)S(1)}, u32[]{:S(2)}, u32[]{:S(2)}) collective-permute-start(s32[4,14]{1,0:T(4,128)S(1)} %pad_add_fusion), channel_id=1, source_target_pairs={{0,8},{4,12},{8,0},{12,4},{1,9},{5,13},{9,1},{13,5},{2,10},{6,14},... | collective-permute-start | bytes 680 | tf_op jit(solution)/shard_map/ppermute | solution.py:675
  18.0 19.8 %collective-permute-start.9 = (bf16[32,1280]{1,0:T(8,128)(2,1)}, bf16[32,1280]{1,0:T(8,128)(2,1)S(1)}, u32[]{:S(2)}, u32[]{:S(2)}) collective-permute-start(bf16[32,1280]{1,0:T(8,128)(2,1)} %get-tuple-element.80), channel_id=1, source_target_pairs={{0,4},{4,8},{8,12},{12,0},{1,5},{5,9},{9,13},{13,1},{2,6},{6,10},{... | collective-permute-start | bytes 245768 | tf_op jit(solution)/shard_map/ppermute | solution.py:675
  18.9 19.0 %collective-permute-start.10 = (bf16[32,1280]{1,0:T(8,128)(2,1)}, bf16[32,1280]{1,0:T(8,128)(2,1)}, u32[]{:S(2)}, u32[]{:S(2)}) collective-permute-start(bf16[32,1280]{1,0:T(8,128)(2,1)} %get-tuple-element.81), channel_id=1, source_target_pairs={{0,8},{4,12},{8,0},{12,4},{1,9},{5,13},{9,1},{13,5},{2,10},{6,14},... | collective-permute-start | bytes 245768 | tf_op jit(solution)/shard_map/ppermute | solution.py:675
  19.5 18.4 %collective-permute-start.11 = (bf16[32,1280]{1,0:T(8,128)(2,1)}, bf16[32,1280]{1,0:T(8,128)(2,1)}, u32[]{:S(2)}, u32[]{:S(2)}) collective-permute-start(bf16[32,1280]{1,0:T(8,128)(2,1)} %get-tuple-element.82), channel_id=1, source_target_pairs={{0,12},{4,0},{8,4},{12,8},{1,13},{5,1},{9,5},{13,9},{2,14},{6,2},{... | collective-permute-start | bytes 245768 | tf_op jit(solution)/shard_map/ppermute | solution.py:675
  22.9 10.4 %collective-permute-start.5 = (bf16[1280,128]{1,0:T(8,128)(2,1)}, bf16[1280,128]{1,0:T(8,128)(2,1)S(1)}, u32[]{:S(2)}, u32[]{:S(2)}) collective-permute-start(bf16[1280,128]{1,0:T(8,128)(2,1)} %dynamic-slice_bitcast_fusion.1), channel_id=1, source_target_pairs={{0,16},{16,0},{1,17},{17,1},{2,18},{18,2},{3,19},{19,3},{4,20},{20... | collective-permute-start | bytes 983048 | tf_op jit(solution)/shard_map/ppermute | solution.py:670
  23.5 13.3 %collective-permute-start.6 = (bf16[128,1280]{1,0:T(8,128)(2,1)S(1)}, bf16[128,1280]{1,0:T(8,128)(2,1)S(1)}, u32[]{:S(2)}, u32[]{:S(2)}) collective-permute-start(bf16[128,1280]{1,0:T(8,128)(2,1)S(1)} %dynamic-slice_bitcast_fusion), channel_id=1, source_target_pairs={{0,16},{16,0},{1,17},{17,1},{2,18},{18,2},{3,19},{19,3},{4,20},{20... | collective-permute-start | bytes 983048 | tf_op jit(solution)/shard_map/ppermute | solution.py:670
  40.1 11.7 %collective-permute-start.12 = (bf16[32,1280]{1,0:T(8,128)(2,1)S(1)}, bf16[32,1280]{1,0:T(8,128)(2,1)S(1)}, u32[]{:S(2)}, u32[]{:S(2)}) collective-permute-start(bf16[32,1280]{1,0:T(8,128)(2,1)S(1)} %get-tuple-element.84), channel_id=1, source_target_pairs={{0,12},{4,0},{8,4},{12,8},{1,13},{5,1},{9,5},{13,9},{2,14},{6,2},{... | collective-permute-start | bytes 245768 | tf_op jit(solution)/shard_map/ppermute | solution.py:675
  40.6 11.1 %collective-permute-start.13 = (bf16[32,1280]{1,0:T(8,128)(2,1)S(1)}, bf16[32,1280]{1,0:T(8,128)(2,1)S(1)}, u32[]{:S(2)}, u32[]{:S(2)}) collective-permute-start(bf16[32,1280]{1,0:T(8,128)(2,1)S(1)} %get-tuple-element.85), channel_id=1, source_target_pairs={{0,8},{4,12},{8,0},{12,4},{1,9},{5,13},{9,1},{13,5},{2,10},{6,14},... | collective-permute-start | bytes 245768 | tf_op jit(solution)/shard_map/ppermute | solution.py:675
  42.1 9.6 %collective-permute-start.14 = (bf16[32,1280]{1,0:T(8,128)(2,1)S(1)}, bf16[32,1280]{1,0:T(8,128)(2,1)S(1)}, u32[]{:S(2)}, u32[]{:S(2)}) collective-permute-start(bf16[32,1280]{1,0:T(8,128)(2,1)S(1)} %get-tuple-element.86), channel_id=1, source_target_pairs={{0,4},{4,8},{8,12},{12,0},{1,5},{5,9},{9,13},{13,1},{2,6},{6,10},{... | collective-permute-start | bytes 245768 | tf_op jit(solution)/shard_map/ppermute | solution.py:675
  54.4 8.8 %collective-permute-start.16 = (bf16[32,1280]{1,0:T(8,128)(2,1)}, bf16[32,1280]{1,0:T(8,128)(2,1)S(1)}, u32[]{:S(2)}, u32[]{:S(2)}) collective-permute-start(bf16[32,1280]{1,0:T(8,128)(2,1)} %get-tuple-element.95), channel_id=1, source_target_pairs={{0,8},{4,12},{8,0},{12,4},{1,9},{5,13},{9,1},{13,5},{2,10},{6,14},... | collective-permute-start | bytes 245768 | tf_op jit(solution)/shard_map/ppermute | solution.py:675
  75.4 22.3 %collective-permute-start.22 = (bf16[96,1280]{1,0:T(8,128)(2,1)S(1)}, bf16[96,1280]{1,0:T(8,128)(2,1)}, u32[]{:S(2)}, u32[]{:S(2)}) collective-permute-start(bf16[96,1280]{1,0:T(8,128)(2,1)S(1)} %shard_map.137.refs_0_), channel_id=1, source_target_pairs={{0,4},{4,8},{8,12},{1,5},{5,9},{9,13},{2,6},{6,10},{10,14},{3,7},{... | collective-permute-start | bytes 737288 | tf_op jit(solution)/shard_map/ppermute | solution.py:684
  78.1 21.0 %collective-permute-start.21 = (bf16[96,1280]{1,0:T(8,128)(2,1)S(1)}, bf16[96,1280]{1,0:T(8,128)(2,1)}, u32[]{:S(2)}, u32[]{:S(2)}) collective-permute-start(bf16[96,1280]{1,0:T(8,128)(2,1)S(1)} %shard_map.137.refs_0_), channel_id=1, source_target_pairs={{4,0},{8,4},{12,8},{5,1},{9,5},{13,9},{6,2},{10,6},{14,10},{7,3},{... | collective-permute-start | bytes 737288 | tf_op jit(solution)/shard_map/ppermute | solution.py:683
  79.4 12.0 %collective-permute-start.29 = (bf16[32,1280]{1,0:T(8,128)(2,1)S(1)}, bf16[32,1280]{1,0:T(8,128)(2,1)S(1)}, u32[]{:S(2)}, u32[]{:S(2)}) collective-permute-start(bf16[32,1280]{1,0:T(8,128)(2,1)S(1)} %copy-done.15), channel_id=1, source_target_pairs={{0,4},{4,8},{8,12},{12,0},{1,5},{5,9},{9,13},{13,1},{2,6},{6,10},{... | collective-permute-start | bytes 245768 | tf_op jit(solution)/shard_map/ppermute | solution.py:675
  82.1 12.0 %collective-permute-start.30 = (bf16[32,1280]{1,0:T(8,128)(2,1)S(1)}, bf16[32,1280]{1,0:T(8,128)(2,1)S(1)}, u32[]{:S(2)}, u32[]{:S(2)}) collective-permute-start(bf16[32,1280]{1,0:T(8,128)(2,1)S(1)} %copy-done.13), channel_id=1, source_target_pairs={{0,8},{4,12},{8,0},{12,4},{1,9},{5,13},{9,1},{13,5},{2,10},{6,14},... | collective-permute-start | bytes 245768 | tf_op jit(solution)/shard_map/ppermute | solution.py:675
  84.4 9.7 %collective-permute-start.31 = (bf16[32,1280]{1,0:T(8,128)(2,1)S(1)}, bf16[32,1280]{1,0:T(8,128)(2,1)S(1)}, u32[]{:S(2)}, u32[]{:S(2)}) collective-permute-start(bf16[32,1280]{1,0:T(8,128)(2,1)S(1)} %copy-done.11), channel_id=1, source_target_pairs={{0,12},{4,0},{8,4},{12,8},{1,13},{5,1},{9,5},{13,9},{2,14},{6,2},{... | collective-permute-start | bytes 245768 | tf_op jit(solution)/shard_map/ppermute | solution.py:675
  97.7 32.0 %collective-permute-start.24 = (bf16[96,1280]{1,0:T(8,128)(2,1)}, bf16[96,1280]{1,0:T(8,128)(2,1)}, u32[]{:S(2)}, u32[]{:S(2)}) collective-permute-start(bf16[96,1280]{1,0:T(8,128)(2,1)} %collective-permute-done.22.refs_2_), channel_id=1, source_target_pairs={{4,8},{8,12},{5,9},{9,13},{6,10},{10,14},{7,11},{11,15},{20,24},{2... | collective-permute-start | bytes 737288 | tf_op jit(solution)/shard_map/ppermute | solution.py:690
  99.1 30.7 %collective-permute-start.23 = (bf16[96,1280]{1,0:T(8,128)(2,1)}, bf16[96,1280]{1,0:T(8,128)(2,1)}, u32[]{:S(2)}, u32[]{:S(2)}) collective-permute-start(bf16[96,1280]{1,0:T(8,128)(2,1)} %collective-permute-done.21.refs_1_), channel_id=1, source_target_pairs={{4,0},{8,4},{5,1},{9,5},{6,2},{10,6},{7,3},{11,7},{20,16},{24,20},... | collective-permute-start | bytes 737288 | tf_op jit(solution)/shard_map/ppermute | solution.py:689
  107.2 8.9 %collective-permute-start.36 = (bf16[32,1280]{1,0:T(8,128)(2,1)S(1)}, bf16[32,1280]{1,0:T(8,128)(2,1)S(1)}, u32[]{:S(2)}, u32[]{:S(2)}) collective-permute-start(bf16[32,1280]{1,0:T(8,128)(2,1)S(1)} %get-tuple-element.112), channel_id=1, source_target_pairs={{0,8},{4,12},{8,0},{12,4},{1,9},{5,13},{9,1},{13,5},{2,10},{6,14},... | collective-permute-start | bytes 245768 | tf_op jit(solution)/shard_map/ppermute | solution.py:675
  128.4 10.7 %collective-permute-start.41 = (bf16[96,1280]{1,0:T(8,128)(2,1)S(1)}, bf16[96,1280]{1,0:T(8,128)(2,1)S(1)}, u32[]{:S(2)}, u32[]{:S(2)}) collective-permute-start(bf16[96,1280]{1,0:T(8,128)(2,1)S(1)} %shard_map.142.refs_0_), channel_id=1, source_target_pairs={{4,0},{8,4},{12,8},{5,1},{9,5},{13,9},{6,2},{10,6},{14,10},{7,3},{... | collective-permute-start | bytes 737288 | tf_op jit(solution)/shard_map/ppermute | solution.py:683
  142.0 11.0 %collective-permute-start.25 = (bf16[96,1280]{1,0:T(8,128)(2,1)S(1)}, bf16[96,1280]{1,0:T(8,128)(2,1)S(1)}, u32[]{:S(2)}, u32[]{:S(2)}) collective-permute-start(bf16[96,1280]{1,0:T(8,128)(2,1)S(1)} %broadcast_select_fusion.1.refs_3_), channel_id=1, source_target_pairs={{4,0},{8,12},{5,1},{9,13},{6,2},{10,14},{7,3},{11,15},{20,16},{24,... | collective-permute-start | bytes 737288 | tf_op jit(solution)/shard_map/ppermute | solution.py:695
  164.2 8.4 %collective-permute-start.45 = (bf16[96,1280]{1,0:T(8,128)(2,1)S(1)}, bf16[96,1280]{1,0:T(8,128)(2,1)S(1)}, u32[]{:S(2)}, u32[]{:S(2)}) collective-permute-start(bf16[96,1280]{1,0:T(8,128)(2,1)S(1)} %broadcast_select_fusion.refs_3_), channel_id=1, source_target_pairs={{4,0},{8,12},{5,1},{9,13},{6,2},{10,14},{7,3},{11,15},{20,16},{24,... | collective-permute-start | bytes 737288 | tf_op jit(solution)/shard_map/ppermute | solution.py:695
  166.4 18.9 %collective-permute-start.28 = (f32[4,16,96]{2,1,0:T(8,128)}, f32[4,16,96]{2,1,0:T(8,128)S(1)}, u32[]{:S(2)}, u32[]{:S(2)}) collective-permute-start(f32[4,16,96]{2,1,0:T(8,128)} %get-tuple-element.101.refs_0_), channel_id=1, source_target_pairs={{0,4},{4,8},{8,12},{12,0},{1,5},{5,9},{9,13},{13,1},{2,6},{6,10},{... | collective-permute-start | bytes 73736 | tf_op jit(solution)/shard_map/ppermute | solution.py:675
  169.1 19.1 %collective-permute-start.27 = (f32[4,16,96]{2,1,0:T(8,128)}, f32[4,16,96]{2,1,0:T(8,128)S(1)}, u32[]{:S(2)}, u32[]{:S(2)}) collective-permute-start(f32[4,16,96]{2,1,0:T(8,128)} %get-tuple-element.101.refs_0_), channel_id=1, source_target_pairs={{0,8},{4,12},{8,0},{12,4},{1,9},{5,13},{9,1},{13,5},{2,10},{6,14},... | collective-permute-start | bytes 73736 | tf_op jit(solution)/shard_map/ppermute | solution.py:675
  169.1 19.1 %collective-permute-start.26 = (f32[4,16,96]{2,1,0:T(8,128)}, f32[4,16,96]{2,1,0:T(8,128)S(1)}, u32[]{:S(2)}, u32[]{:S(2)}) collective-permute-start(f32[4,16,96]{2,1,0:T(8,128)} %get-tuple-element.101.refs_0_), channel_id=1, source_target_pairs={{0,12},{4,0},{8,4},{12,8},{1,13},{5,1},{9,5},{13,9},{2,14},{6,2},{... | collective-permute-start | bytes 73736 | tf_op jit(solution)/shard_map/ppermute | solution.py:675
  220.2 8.6 %collective-permute-start.50 = (bf16[512,1280]{1,0:T(8,128)(2,1)}, bf16[512,1280]{1,0:T(8,128)(2,1)S(1)}, u32[]{:S(2)}, u32[]{:S(2)}) collective-permute-start(bf16[512,1280]{1,0:T(8,128)(2,1)} %shard_map.148), channel_id=1, source_target_pairs={{0,1},{1,0},{2,3},{3,2},{4,5},{5,4},{6,7},{7,6},{8,9},{9,8},{10,11... | collective-permute-start | bytes 3932168 | tf_op jit(solution)/shard_map/ppermute | solution.py:670
  220.8 16.7 %collective-permute-start.53 = (bf16[256,1280]{1,0:T(8,128)(2,1)S(1)}, bf16[256,1280]{1,0:T(8,128)(2,1)S(1)}, u32[]{:S(2)}, u32[]{:S(2)}) collective-permute-start(bf16[256,1280]{1,0:T(8,128)(2,1)S(1)} %get-tuple-element.140), channel_id=1, source_target_pairs={{0,2},{2,0},{1,3},{3,1},{4,6},{6,4},{5,7},{7,5},{8,10},{10,8},{9,1... | collective-permute-start | bytes 1966088 | tf_op jit(solution)/shard_map/ppermute | solution.py:670
  222.4 16.4 %collective-permute-start.51 = (bf16[256,1280]{1,0:T(8,128)(2,1)S(1)}, bf16[256,1280]{1,0:T(8,128)(2,1)S(1)}, u32[]{:S(2)}, u32[]{:S(2)}) collective-permute-start(bf16[256,1280]{1,0:T(8,128)(2,1)S(1)} %get-tuple-element.141), channel_id=1, source_target_pairs={{0,16},{16,0},{1,17},{17,1},{2,18},{18,2},{3,19},{19,3},{4,20},{20... | collective-permute-start | bytes 1966088 | tf_op jit(solution)/shard_map/ppermute | solution.py:670
  239.1 8.5 %collective-permute-start.52 = (bf16[128,1280]{1,0:T(8,128)(2,1)S(1)}, bf16[128,1280]{1,0:T(8,128)(2,1)S(1)}, u32[]{:S(2)}, u32[]{:S(2)}) collective-permute-start(bf16[128,1280]{1,0:T(8,128)(2,1)S(1)} %constant_dynamic-slice_fusion.2), channel_id=1, source_target_pairs={{0,2},{2,0},{1,3},{3,1},{4,6},{6,4},{5,7},{7,5},{8,10},{10,8},{9,1... | collective-permute-start | bytes 983048 | tf_op jit(solution)/shard_map/ppermute | solution.py:670
  248.2 14.4 %collective-permute-start.56 = (bf16[256,1280]{1,0:T(8,128)(2,1)S(1)}, bf16[256,1280]{1,0:T(8,128)(2,1)S(1)}, u32[]{:S(2)}, u32[]{:S(2)}) collective-permute-start(bf16[256,1280]{1,0:T(8,128)(2,1)S(1)} %pad_maximum_fusion), channel_id=1, source_target_pairs={{0,2},{2,0},{1,3},{3,1},{4,6},{6,4},{5,7},{7,5},{8,10},{10,8},{9,1... | collective-permute-start | bytes 1966088 | tf_op jit(solution)/shard_map/ppermute | solution.py:670
  249.8 15.7 %collective-permute-start.55 = (bf16[256,1280]{1,0:T(8,128)(2,1)S(1)}, bf16[256,1280]{1,0:T(8,128)(2,1)S(1)}, u32[]{:S(2)}, u32[]{:S(2)}) collective-permute-start(bf16[256,1280]{1,0:T(8,128)(2,1)S(1)} %pad_maximum_fusion), channel_id=1, source_target_pairs={{0,16},{16,0},{1,17},{17,1},{2,18},{18,2},{3,19},{19,3},{4,20},{20... | collective-permute-start | bytes 1966088 | tf_op jit(solution)/shard_map/ppermute | solution.py:670
  251.2 14.5 %collective-permute-start.59 = (bf16[256,1280]{1,0:T(8,128)(2,1)S(1)}, bf16[256,1280]{1,0:T(8,128)(2,1)S(1)}, u32[]{:S(2)}, u32[]{:S(2)}) collective-permute-start(bf16[256,1280]{1,0:T(8,128)(2,1)S(1)} %pad_maximum_fusion), channel_id=1, source_target_pairs={{0,1},{1,0},{2,3},{3,2},{4,5},{5,4},{6,7},{7,6},{8,9},{9,8},{10,11... | collective-permute-start | bytes 1966088 | tf_op jit(solution)/shard_map/ppermute | solution.py:670
  263.3 10.2 %collective-permute-start.61 = (bf16[256,1280]{1,0:T(8,128)(2,1)S(1)}, bf16[256,1280]{1,0:T(8,128)(2,1)S(1)}, u32[]{:S(2)}, u32[]{:S(2)}) collective-permute-start(bf16[256,1280]{1,0:T(8,128)(2,1)S(1)} %collective-permute-done.56), channel_id=1, source_target_pairs={{0,1},{1,0},{2,3},{3,2},{4,5},{5,4},{6,7},{7,6},{8,9},{9,8},{10,11... | collective-permute-start | bytes 1966088 | tf_op jit(solution)/shard_map/ppermute | solution.py:670
  (69 other events, 642.3 us)
